TPU v7x, 32 devices: a whole 2x2x4 slice. The times are simulated.
32 devices in a mesh: pts: 8 (over z, core), orb: 4 (over y, x).
Axes of the slice: x: 2, y: 2, z: 4, core: 2. Of those that a mesh axis runs over, the one named last changes fastest.
Arguments:
- phi_occ: bfloat16 [768, 2048], P('pts', 'orb'), may hold values from -0.75 to 0.75
- phi_vir: bfloat16 [768, 20480], P('pts', 'orb'), may hold values from -0.5 to 0.5
- eps_occ: float32 [2048], P('orb'), may hold values from -1 to -0.2
- eps_vir: float32 [20480], P('orb'), may hold values from 0.02 to 1.5
- taus: float32 [2], replicated, may hold values from 0.5 to 3
- pair_mask: int32 [8, 8], P('pts'), may hold values 0 or 1
- basis: bfloat16 [768, 4096], P('pts', 'orb'), may hold values from -0.375 to 0.375
Outputs:
- aux_response: float32 [4096, 2, 4096], P('pts', None, 'orb')
All inputs are finite; a program needn't handle non-finite values. No bound on the sum of `pair_mask` on one device may be relied on, other than what follows from the above.
Results may differ from a plain program's by a relative error of at most 0.0057.
Values may be sent and summed in bfloat16 or wider, within the bound.
A program may use at most 64 MiB of HBM per device.

v0:
```python
import jax
import jax.numpy as jnp
from jax import lax
from jax.sharding import PartitionSpec as P

NOFF = 8


def from_behind(value, axis, steps):
    count = lax.axis_size(axis)
    pairs = [(source, (source + steps) % count) for source in range(count)]
    return lax.ppermute(value, axis, pairs)


def on_device(phi_occ, phi_vir, eps_occ, eps_vir, taus, pair_mask, basis):
    half = NOFF // 2
    expo_occ = jnp.exp(taus[:, None] * eps_occ[None, :])
    expo_vir = jnp.exp(-taus[:, None] * eps_vir[None, :])
    weighted_occ = (phi_occ.astype(jnp.float32)[None] * expo_occ[:, None, :]).astype(jnp.bfloat16)
    weighted_vir = (phi_vir.astype(jnp.float32)[None] * expo_vir[:, None, :]).astype(jnp.bfloat16)
    factors = pair_mask[0].astype(jnp.float32)

    def pair_block(slot, panels):
        occ_part, vir_part, basis_part = panels
        g_occ = jnp.einsum(
            "tro,co->trc", weighted_occ, occ_part, preferred_element_type=jnp.float32
        )
        g_vir = jnp.einsum(
            "tra,ca->trc", weighted_vir, vir_part, preferred_element_type=jnp.float32
        )
        g_occ, g_vir = lax.psum((g_occ, g_vir), "orb")
        chi = (g_occ * g_vir * factors[slot]).astype(jnp.bfloat16)
        return jnp.einsum("trc,cq->trq", chi, basis_part, preferred_element_type=jnp.float32)

    totals = jnp.zeros((taus.shape[0], phi_occ.shape[0], basis.shape[1]), jnp.float32)
    ahead = (phi_occ, phi_vir, basis)
    behind = (phi_occ, phi_vir, basis)
    for step in range(1, half + 1):
        ahead = from_behind((ahead[0], ahead[1], ahead[2]), "pts", -1)
        totals = totals + pair_block(half + step - 1, ahead)
        behind = from_behind((behind[0], behind[1], behind[2]), "pts", 1)
        totals = totals + pair_block(half - step, behind)
    projected = totals.astype(jnp.bfloat16)
    full_basis = lax.all_gather(basis, "orb", axis=1, tiled=True)
    basis_cols = lax.all_to_all(full_basis, "pts", split_axis=1, concat_axis=0, tiled=True)
    return jnp.einsum(
        "rp,trq->ptq",
        basis_cols,
        lax.all_gather(projected, "pts", axis=1, tiled=True),
        preferred_element_type=jnp.float32,
    )


def solution(mesh):
    placed = (
        P("pts", "orb"),
        P("pts", "orb"),
        P("orb"),
        P("orb"),
        P(),
        P("pts", None),
        P("pts", "orb"),
    )
    return jax.shard_map(
        on_device, mesh=mesh, in_specs=placed, out_specs=P("pts", None, "orb"), check_vma=False
    )
```

profile of v0, /device:TPU:0, one launch (start us, length us, event | category | flops | bytes accessed | tf_op | source)
XLA Modules:
  0.0 266.7 jit_solution(18031982958980073584)
XLA Ops:
  6.5 0.5 collective-permute-start.3
  7.0 4.0 %collective-permute-start = (bf16[96,512]{1,0:T(8,128)(2,1)}, bf16[96,512]{1,0:T(8,128)(2,1)S(1)}, u32[]{:S(2)}, u32[]{:S(2)}) collective-permute-start(bf16[96,512]{1,0:T(8,128)(2,1)} %param.7), channel_id=1, source_target_pairs={{0,28},{4,0},{8,4},{12,8},{16,12},{20,16},{24,20},{28,24},{1,29},{... | collective-permute-start | bytes 294920 | tf_op jit(solution)/shard_map/ppermute | solution.py:12
  11.0 3.5 %collective-permute-start.1 = (bf16[96,5120]{1,0:T(8,128)(2,1)}, bf16[96,5120]{1,0:T(8,128)(2,1)S(1)}, u32[]{:S(2)}, u32[]{:S(2)}) collective-permute-start(bf16[96,5120]{1,0:T(8,128)(2,1)} %param.8), channel_id=1, source_target_pairs={{0,28},{4,0},{8,4},{12,8},{16,12},{20,16},{24,20},{28,24},{1,29},{... | collective-permute-start | bytes 2949128 | tf_op jit(solution)/shard_map/ppermute | solution.py:12
  14.6 0.7 neg.4
  15.2 0.8 multiply_exponential_fusion
  16.1 0.8 multiply_exponential_fusion.1
  16.8 0.9 convert_element_type.43
  17.7 1.4 convert_element_type.45
  19.1 0.0 collective-permute-done.3
  19.1 0.1 collective-permute-start.9
  19.2 0.8 fusion.42
  20.0 16.5 %collective-permute-done.4 = bf16[96,5120]{1,0:T(8,128)(2,1)S(1)} collective-permute-done((bf16[96,5120]{1,0:T(8,128)(2,1)}, bf16[96,5120]{1,0:T(8,128)(2,1)S(1)}, u32[]{:S(2)}, u32[]{:S(2)}) %collective-permute-start.4) | collective-permute-done | bytes 983072 | tf_op jit(solution)/shard_map/ppermute | solution.py:12
  36.5 0.9 fusion.43
  37.4 3.5 %collective-permute-start.6 = (bf16[96,512]{1,0:T(8,128)(2,1)S(1)}, bf16[96,512]{1,0:T(8,128)(2,1)S(1)}, u32[]{:S(2)}, u32[]{:S(2)}) collective-permute-start(bf16[96,512]{1,0:T(8,128)(2,1)S(1)} %collective-permute-done), channel_id=1, source_target_pairs={{0,28},{4,0},{8,4},{12,8},{16,12},{20,16},{24,20},{28,24},{1,29},{... | collective-permute-start | bytes 294920 | tf_op jit(solution)/shard_map/ppermute | solution.py:12
  40.9 3.5 %collective-permute-start.7 = (bf16[96,5120]{1,0:T(8,128)(2,1)S(1)}, bf16[96,5120]{1,0:T(8,128)(2,1)S(1)}, u32[]{:S(2)}, u32[]{:S(2)}) collective-permute-start(bf16[96,5120]{1,0:T(8,128)(2,1)S(1)} %collective-permute-done.1), channel_id=1, source_target_pairs={{0,28},{4,0},{8,4},{12,8},{16,12},{20,16},{24,20},{28,24},{1,29},{... | collective-permute-start | bytes 2949128 | tf_op jit(solution)/shard_map/ppermute | solution.py:12
  44.5 0.8 fusion.40
  45.3 0.8 fusion.41
  46.2 2.6 collective-permute-start.12
  48.7 14.2 %collective-permute-done.15 = bf16[96,512]{1,0:T(8,128)(2,1)S(1)} collective-permute-done((bf16[96,512]{1,0:T(8,128)(2,1)S(1)}, bf16[96,512]{1,0:T(8,128)(2,1)S(1)}, u32[]{:S(2)}, u32[]{:S(2)}) %collective-permute-start.15) | collective-permute-done | bytes 98336 | tf_op jit(solution)/shard_map/ppermute | solution.py:12
  63.0 0.8 fusion.38
  63.8 0.8 fusion.39
  64.7 3.5 %collective-permute-start.18 = (bf16[96,512]{1,0:T(8,128)(2,1)S(1)}, bf16[96,512]{1,0:T(8,128)(2,1)S(1)}, u32[]{:S(2)}, u32[]{:S(2)}) collective-permute-start(bf16[96,512]{1,0:T(8,128)(2,1)S(1)} %collective-permute-done.12), channel_id=1, source_target_pairs={{0,28},{4,0},{8,4},{12,8},{16,12},{20,16},{24,20},{28,24},{1,29},{... | collective-permute-start | bytes 294920 | tf_op jit(solution)/shard_map/ppermute | solution.py:12
  68.2 1.1 collective-permute-done.21
  69.3 0.8 fusion.36
  70.1 2.5 collective-permute-start.13
  72.6 0.8 fusion.37
  73.5 1.3 fusion.6
  74.8 1.3 fusion.7
  76.1 16.0 %collective-permute-done.16 = bf16[96,5120]{1,0:T(8,128)(2,1)S(1)} collective-permute-done((bf16[96,5120]{1,0:T(8,128)(2,1)S(1)}, bf16[96,5120]{1,0:T(8,128)(2,1)S(1)}, u32[]{:S(2)}, u32[]{:S(2)}) %collective-permute-start.16) | collective-permute-done | bytes 983072 | tf_op jit(solution)/shard_map/ppermute | solution.py:12
  92.1 1.3 fusion.4
  93.4 3.5 %collective-permute-start.19 = (bf16[96,5120]{1,0:T(8,128)(2,1)S(1)}, bf16[96,5120]{1,0:T(8,128)(2,1)S(1)}, u32[]{:S(2)}, u32[]{:S(2)}) collective-permute-start(bf16[96,5120]{1,0:T(8,128)(2,1)S(1)} %collective-permute-done.13), channel_id=1, source_target_pairs={{0,28},{4,0},{8,4},{12,8},{16,12},{20,16},{24,20},{28,24},{1,29},{... | collective-permute-start | bytes 2949128 | tf_op jit(solution)/shard_map/ppermute | solution.py:12
  96.9 1.3 fusion.5
  98.3 1.3 fusion.2
  99.6 1.3 fusion.3
  100.9 14.9 %collective-permute-done.22 = bf16[96,5120]{1,0:T(8,128)(2,1)S(1)} collective-permute-done((bf16[96,5120]{1,0:T(8,128)(2,1)S(1)}, bf16[96,5120]{1,0:T(8,128)(2,1)S(1)}, u32[]{:S(2)}, u32[]{:S(2)}) %collective-permute-start.22) | collective-permute-done | bytes 983072 | tf_op jit(solution)/shard_map/ppermute | solution.py:12
  115.8 1.3 fusion
  117.1 1.3 fusion.1
  118.4 0.0 all-reduce.3.cloned.1.call-update
  118.4 0.0 all-gather.2.cloned.1.call-start
  118.5 0.1 collective-permute-start.5
  118.5 3.5 %collective-permute-start.2 = (bf16[96,1024]{1,0:T(8,128)(2,1)S(1)}, bf16[96,1024]{1,0:T(8,128)(2,1)S(1)}, u32[]{:S(2)}, u32[]{:S(2)}) collective-permute-start(bf16[96,1024]{1,0:T(8,128)(2,1)S(1)} %copy-done), channel_id=1, source_target_pairs={{0,28},{4,0},{8,4},{12,8},{16,12},{20,16},{24,20},{28,24},{1,29},{... | collective-permute-start | bytes 589832 | tf_op jit(solution)/shard_map/ppermute | solution.py:12
  122.1 3.6 %collective-permute-done.5 = bf16[96,1024]{1,0:T(8,128)(2,1)S(1)} collective-permute-done((bf16[96,1024]{1,0:T(8,128)(2,1)S(1)}, bf16[96,1024]{1,0:T(8,128)(2,1)S(1)}, u32[]{:S(2)}, u32[]{:S(2)}) %collective-permute-start.5) | collective-permute-done | bytes 196640 | tf_op jit(solution)/shard_map/ppermute | solution.py:12
  125.6 3.5 %collective-permute-start.8 = (bf16[96,1024]{1,0:T(8,128)(2,1)S(1)}, bf16[96,1024]{1,0:T(8,128)(2,1)S(1)}, u32[]{:S(2)}, u32[]{:S(2)}) collective-permute-start(bf16[96,1024]{1,0:T(8,128)(2,1)S(1)} %collective-permute-done.2), channel_id=1, source_target_pairs={{0,28},{4,0},{8,4},{12,8},{16,12},{20,16},{24,20},{28,24},{1,29},{... | collective-permute-start | bytes 589832 | tf_op jit(solution)/shard_map/ppermute | solution.py:12
  129.2 3.6 %collective-permute-done.11 = bf16[96,1024]{1,0:T(8,128)(2,1)S(1)} collective-permute-done((bf16[96,1024]{1,0:T(8,128)(2,1)S(1)}, bf16[96,1024]{1,0:T(8,128)(2,1)S(1)}, u32[]{:S(2)}, u32[]{:S(2)}) %collective-permute-start.11) | collective-permute-done | bytes 196640 | tf_op jit(solution)/shard_map/ppermute | solution.py:12
  132.7 3.5 %collective-permute-start.14 = (bf16[96,1024]{1,0:T(8,128)(2,1)S(1)}, bf16[96,1024]{1,0:T(8,128)(2,1)S(1)}, u32[]{:S(2)}, u32[]{:S(2)}) collective-permute-start(bf16[96,1024]{1,0:T(8,128)(2,1)S(1)} %collective-permute-done.8), channel_id=1, source_target_pairs={{0,28},{4,0},{8,4},{12,8},{16,12},{20,16},{24,20},{28,24},{1,29},{... | collective-permute-start | bytes 589832 | tf_op jit(solution)/shard_map/ppermute | solution.py:12
  136.3 0.7 fusion.88
  137.0 2.9 %collective-permute-done.17 = bf16[96,1024]{1,0:T(8,128)(2,1)S(1)} collective-permute-done((bf16[96,1024]{1,0:T(8,128)(2,1)S(1)}, bf16[96,1024]{1,0:T(8,128)(2,1)S(1)}, u32[]{:S(2)}, u32[]{:S(2)}) %collective-permute-start.17) | collective-permute-done | bytes 196640 | tf_op jit(solution)/shard_map/ppermute | solution.py:12
  139.8 3.5 %collective-permute-start.20 = (bf16[96,1024]{1,0:T(8,128)(2,1)S(1)}, bf16[96,1024]{1,0:T(8,128)(2,1)S(1)}, u32[]{:S(2)}, u32[]{:S(2)}) collective-permute-start(bf16[96,1024]{1,0:T(8,128)(2,1)S(1)} %collective-permute-done.14), channel_id=1, source_target_pairs={{0,28},{4,0},{8,4},{12,8},{16,12},{20,16},{24,20},{28,24},{1,29},{... | collective-permute-start | bytes 589832 | tf_op jit(solution)/shard_map/ppermute | solution.py:12
  143.4 38.2 %all-reduce.3.cloned.1.call-done = (f32[2,96,96]{2,1,0:T(8,128)}, f32[2,96,96]{2,1,0:T(8,128)}, f32[2,96,96]{2,1,0:T(8,128)}, f32[2,96,96]{2,1,0:T(8,128)}, f32[...) async-done(((f32[2,96,96]{2,1,0:T(8,128)}, ...) | async-done | bytes 1179664 | tf_op jit(solution)/shard_map/psum | solution.py:31
  181.6 1.9 fusion.47
  183.5 1.8 fusion.50
  185.3 0.9 fusion.53
  186.2 0.9 convolution_add_fusion.3
  187.1 1.0 fusion.26
  188.1 1.0 fusion.25
  189.1 0.9 fusion.44
  190.0 1.6 fusion.27
  191.6 0.0 all-gather.2.cloned.1.call-update
  191.6 11.2 %all_gather.7 = bf16[96,4096]{1,0:T(8,128)(2,1)S(1)} all-gather(bf16[96,1024]{1,0:T(8,128)(2,1)S(1)} %copy-done), channel_id=1, replica_groups=mesh['pts'=8,'orb'=4] {'orb'}, dimensions={1}, use_global_device_ids=true | all-gather | bytes 983040 | tf_op jit(solution)/shard_map/all_gather | solution.py:44
  202.8 0.1 copy.12
  202.9 42.4 %all_to_all.19 = bf16[96,8,512]{2,0,1:T(8,128)(2,1)S(1)} all-to-all(bf16[96,8,512]{2,0,1:T(8,128)(2,1)S(1)} %bitcast.93), channel_id=1, replica_groups=mesh['pts'=8,'orb'=4] {'pts'}, dimensions={1} | all-to-all | bytes 1572864 | tf_op jit(solution)/shard_map/all_to_all | solution.py:45
  245.3 1.6 all-gather.2.cloned.1.call-done
  246.9 5.7 %convolution_bitcast_fusion = f32[512,2,1024]{0,2,1:T(8,128)} fusion(bf16[2,768,1024]{2,1,0:T(8,128)(2,1)} %all-gather.2.cloned.1.call-done, bf16[768,512,1]{1,0,2:T(8,128)(2,1)S(1)} %bitcast.95), kind=kOutput, calls=%fused_computation.9 | convolution fusion | flops 1610612736 | bytes 8126464 | tf_op jit(solution)/shard_map/rp,trq->ptq/dot_general | solution.py:46
  252.6 7.3 %copy.9 = f32[512,2,1024]{2,1,0:T(2,128)} copy(f32[512,2,1024]{0,2,1:T(8,128)} %convolution_bitcast_fusion) | data formatting | bytes 8388608 | tf_op jit(solution)/shard_map/rp,trq->ptq/dot_general | solution.py:46
  (54 shorter events, 0.1 us)
Async XLA Ops:
  6.5 175.1 %all-reduce.3.cloned.1.call-start = ((), (), s32[]{:S(2)}) async-start(), calls=%async_computation.2 | async-start | bytes 3145728 | tf_op jit(solution)/shard_map/psum | solution.py:31
  6.5 12.6 %collective-permute-start.3 = (bf16[96,512]{1,0:T(8,128)(2,1)}, bf16[96,512]{1,0:T(8,128)(2,1)S(1)}, u32[]{:S(2)}, u32[]{:S(2)}) collective-permute-start(bf16[96,512]{1,0:T(8,128)(2,1)} %param.7), channel_id=1, source_target_pairs={{0,4},{4,8},{8,12},{12,16},{16,20},{20,24},{24,28},{28,0},{1,5},{5... | collective-permute-start | bytes 294920 | tf_op jit(solution)/shard_map/ppermute | solution.py:12
  7.0 29.6 %collective-permute-start = (bf16[96,512]{1,0:T(8,128)(2,1)}, bf16[96,512]{1,0:T(8,128)(2,1)S(1)}, u32[]{:S(2)}, u32[]{:S(2)}) collective-permute-start(bf16[96,512]{1,0:T(8,128)(2,1)} %param.7), channel_id=1, source_target_pairs={{0,28},{4,0},{8,4},{12,8},{16,12},{20,16},{24,20},{28,24},{1,29},{... | collective-permute-start | bytes 294920 | tf_op jit(solution)/shard_map/ppermute | solution.py:12
  11.0 25.5 %collective-permute-start.4 = (bf16[96,5120]{1,0:T(8,128)(2,1)}, bf16[96,5120]{1,0:T(8,128)(2,1)S(1)}, u32[]{:S(2)}, u32[]{:S(2)}) collective-permute-start(bf16[96,5120]{1,0:T(8,128)(2,1)} %param.8), channel_id=1, source_target_pairs={{0,4},{4,8},{8,12},{12,16},{16,20},{20,24},{24,28},{28,0},{1,5},{5... | collective-permute-start | bytes 2949128 | tf_op jit(solution)/shard_map/ppermute | solution.py:12
  11.0 29.9 %collective-permute-start.1 = (bf16[96,5120]{1,0:T(8,128)(2,1)}, bf16[96,5120]{1,0:T(8,128)(2,1)S(1)}, u32[]{:S(2)}, u32[]{:S(2)}) collective-permute-start(bf16[96,5120]{1,0:T(8,128)(2,1)} %param.8), channel_id=1, source_target_pairs={{0,28},{4,0},{8,4},{12,8},{16,12},{20,16},{24,20},{28,24},{1,29},{... | collective-permute-start | bytes 2949128 | tf_op jit(solution)/shard_map/ppermute | solution.py:12
  19.1 21.8 %collective-permute-start.9 = (bf16[96,512]{1,0:T(8,128)(2,1)S(1)}, bf16[96,512]{1,0:T(8,128)(2,1)S(1)}, u32[]{:S(2)}, u32[]{:S(2)}) collective-permute-start(bf16[96,512]{1,0:T(8,128)(2,1)S(1)} %collective-permute-done.3), channel_id=1, source_target_pairs={{0,4},{4,8},{8,12},{12,16},{16,20},{20,24},{24,28},{28,0},{1,5},{5... | collective-permute-start | bytes 294920 | tf_op jit(solution)/shard_map/ppermute | solution.py:12
  36.5 31.7 %collective-permute-start.10 = (bf16[96,5120]{1,0:T(8,128)(2,1)S(1)}, bf16[96,5120]{1,0:T(8,128)(2,1)S(1)}, u32[]{:S(2)}, u32[]{:S(2)}) collective-permute-start(bf16[96,5120]{1,0:T(8,128)(2,1)S(1)} %collective-permute-done.4), channel_id=1, source_target_pairs={{0,4},{4,8},{8,12},{12,16},{16,20},{20,24},{24,28},{28,0},{1,5},{5... | collective-permute-start | bytes 2949128 | tf_op jit(solution)/shard_map/ppermute | solution.py:12
  37.4 7.9 %collective-permute-start.6 = (bf16[96,512]{1,0:T(8,128)(2,1)S(1)}, bf16[96,512]{1,0:T(8,128)(2,1)S(1)}, u32[]{:S(2)}, u32[]{:S(2)}) collective-permute-start(bf16[96,512]{1,0:T(8,128)(2,1)S(1)} %collective-permute-done), channel_id=1, source_target_pairs={{0,28},{4,0},{8,4},{12,8},{16,12},{20,16},{24,20},{28,24},{1,29},{... | collective-permute-start | bytes 294920 | tf_op jit(solution)/shard_map/ppermute | solution.py:12
  40.9 22.0 %collective-permute-start.15 = (bf16[96,512]{1,0:T(8,128)(2,1)S(1)}, bf16[96,512]{1,0:T(8,128)(2,1)S(1)}, u32[]{:S(2)}, u32[]{:S(2)}) collective-permute-start(bf16[96,512]{1,0:T(8,128)(2,1)S(1)} %collective-permute-done.9), channel_id=1, source_target_pairs={{0,4},{4,8},{8,12},{12,16},{16,20},{20,24},{24,28},{28,0},{1,5},{5... | collective-permute-start | bytes 294920 | tf_op jit(solution)/shard_map/ppermute | solution.py:12
  40.9 29.2 %collective-permute-start.7 = (bf16[96,5120]{1,0:T(8,128)(2,1)S(1)}, bf16[96,5120]{1,0:T(8,128)(2,1)S(1)}, u32[]{:S(2)}, u32[]{:S(2)}) collective-permute-start(bf16[96,5120]{1,0:T(8,128)(2,1)S(1)} %collective-permute-done.1), channel_id=1, source_target_pairs={{0,28},{4,0},{8,4},{12,8},{16,12},{20,16},{24,20},{28,24},{1,29},{... | collective-permute-start | bytes 2949128 | tf_op jit(solution)/shard_map/ppermute | solution.py:12
  46.2 17.6 %collective-permute-start.12 = (bf16[96,512]{1,0:T(8,128)(2,1)S(1)}, bf16[96,512]{1,0:T(8,128)(2,1)S(1)}, u32[]{:S(2)}, u32[]{:S(2)}) collective-permute-start(bf16[96,512]{1,0:T(8,128)(2,1)S(1)} %collective-permute-done.6), channel_id=1, source_target_pairs={{0,28},{4,0},{8,4},{12,8},{16,12},{20,16},{24,20},{28,24},{1,29},{... | collective-permute-start | bytes 294920 | tf_op jit(solution)/shard_map/ppermute | solution.py:12
  63.0 6.3 %collective-permute-start.21 = (bf16[96,512]{1,0:T(8,128)(2,1)S(1)}, bf16[96,512]{1,0:T(8,128)(2,1)S(1)}, u32[]{:S(2)}, u32[]{:S(2)}) collective-permute-start(bf16[96,512]{1,0:T(8,128)(2,1)S(1)} %collective-permute-done.15), channel_id=1, source_target_pairs={{0,4},{4,8},{8,12},{12,16},{16,20},{20,24},{24,28},{28,0},{1,5},{5... | collective-permute-start | bytes 294920 | tf_op jit(solution)/shard_map/ppermute | solution.py:12
  64.7 7.9 %collective-permute-start.18 = (bf16[96,512]{1,0:T(8,128)(2,1)S(1)}, bf16[96,512]{1,0:T(8,128)(2,1)S(1)}, u32[]{:S(2)}, u32[]{:S(2)}) collective-permute-start(bf16[96,512]{1,0:T(8,128)(2,1)S(1)} %collective-permute-done.12), channel_id=1, source_target_pairs={{0,28},{4,0},{8,4},{12,8},{16,12},{20,16},{24,20},{28,24},{1,29},{... | collective-permute-start | bytes 294920 | tf_op jit(solution)/shard_map/ppermute | solution.py:12
  68.2 23.9 %collective-permute-start.16 = (bf16[96,5120]{1,0:T(8,128)(2,1)S(1)}, bf16[96,5120]{1,0:T(8,128)(2,1)S(1)}, u32[]{:S(2)}, u32[]{:S(2)}) collective-permute-start(bf16[96,5120]{1,0:T(8,128)(2,1)S(1)} %collective-permute-done.10), channel_id=1, source_target_pairs={{0,4},{4,8},{8,12},{12,16},{16,20},{20,24},{24,28},{28,0},{1,5},{5... | collective-permute-start | bytes 2949128 | tf_op jit(solution)/shard_map/ppermute | solution.py:12
  70.1 23.3 %collective-permute-start.13 = (bf16[96,5120]{1,0:T(8,128)(2,1)S(1)}, bf16[96,5120]{1,0:T(8,128)(2,1)S(1)}, u32[]{:S(2)}, u32[]{:S(2)}) collective-permute-start(bf16[96,5120]{1,0:T(8,128)(2,1)S(1)} %collective-permute-done.7), channel_id=1, source_target_pairs={{0,28},{4,0},{8,4},{12,8},{16,12},{20,16},{24,20},{28,24},{1,29},{... | collective-permute-start | bytes 2949128 | tf_op jit(solution)/shard_map/ppermute | solution.py:12
  92.1 23.7 %collective-permute-start.22 = (bf16[96,5120]{1,0:T(8,128)(2,1)S(1)}, bf16[96,5120]{1,0:T(8,128)(2,1)S(1)}, u32[]{:S(2)}, u32[]{:S(2)}) collective-permute-start(bf16[96,5120]{1,0:T(8,128)(2,1)S(1)} %collective-permute-done.16), channel_id=1, source_target_pairs={{0,4},{4,8},{8,12},{12,16},{16,20},{20,24},{24,28},{28,0},{1,5},{5... | collective-permute-start | bytes 2949128 | tf_op jit(solution)/shard_map/ppermute | solution.py:12
  93.4 23.7 %collective-permute-start.19 = (bf16[96,5120]{1,0:T(8,128)(2,1)S(1)}, bf16[96,5120]{1,0:T(8,128)(2,1)S(1)}, u32[]{:S(2)}, u32[]{:S(2)}) collective-permute-start(bf16[96,5120]{1,0:T(8,128)(2,1)S(1)} %collective-permute-done.13), channel_id=1, source_target_pairs={{0,28},{4,0},{8,4},{12,8},{16,12},{20,16},{24,20},{28,24},{1,29},{... | collective-permute-start | bytes 2949128 | tf_op jit(solution)/shard_map/ppermute | solution.py:12
  117.1 1.4 copy-start
  117.1 19.2 %copy-start.13 = (s32[1,8]{1,0:T(1,128)S(1)}, s32[1,8]{1,0:T(1,128)}, u32[]{:S(2)}) copy-start(s32[1,8]{1,0:T(1,128)} %param.12) | copy-start | bytes 100
  118.4 128.4 %all-gather.2.cloned.1.call-start = ((), (), s32[]{:S(2)}) async-start(), calls=%async_computation.1 | async-start | bytes 3538944 | tf_op jit(solution)/shard_map/all_gather | solution.py:49
  118.5 7.2 %collective-permute-start.5 = (bf16[96,1024]{1,0:T(8,128)(2,1)S(1)}, bf16[96,1024]{1,0:T(8,128)(2,1)S(1)}, u32[]{:S(2)}, u32[]{:S(2)}) collective-permute-start(bf16[96,1024]{1,0:T(8,128)(2,1)S(1)} %copy-done), channel_id=1, source_target_pairs={{0,4},{4,8},{8,12},{12,16},{16,20},{20,24},{24,28},{28,0},{1,5},{5... | collective-permute-start | bytes 589832 | tf_op jit(solution)/shard_map/ppermute | solution.py:12
  118.5 7.1 %collective-permute-start.2 = (bf16[96,1024]{1,0:T(8,128)(2,1)S(1)}, bf16[96,1024]{1,0:T(8,128)(2,1)S(1)}, u32[]{:S(2)}, u32[]{:S(2)}) collective-permute-start(bf16[96,1024]{1,0:T(8,128)(2,1)S(1)} %copy-done), channel_id=1, source_target_pairs={{0,28},{4,0},{8,4},{12,8},{16,12},{20,16},{24,20},{28,24},{1,29},{... | collective-permute-start | bytes 589832 | tf_op jit(solution)/shard_map/ppermute | solution.py:12
  125.6 7.1 %collective-permute-start.11 = (bf16[96,1024]{1,0:T(8,128)(2,1)S(1)}, bf16[96,1024]{1,0:T(8,128)(2,1)S(1)}, u32[]{:S(2)}, u32[]{:S(2)}) collective-permute-start(bf16[96,1024]{1,0:T(8,128)(2,1)S(1)} %collective-permute-done.5), channel_id=1, source_target_pairs={{0,4},{4,8},{8,12},{12,16},{16,20},{20,24},{24,28},{28,0},{1,5},{5... | collective-permute-start | bytes 589832 | tf_op jit(solution)/shard_map/ppermute | solution.py:12
  125.6 7.1 %collective-permute-start.8 = (bf16[96,1024]{1,0:T(8,128)(2,1)S(1)}, bf16[96,1024]{1,0:T(8,128)(2,1)S(1)}, u32[]{:S(2)}, u32[]{:S(2)}) collective-permute-start(bf16[96,1024]{1,0:T(8,128)(2,1)S(1)} %collective-permute-done.2), channel_id=1, source_target_pairs={{0,28},{4,0},{8,4},{12,8},{16,12},{20,16},{24,20},{28,24},{1,29},{... | collective-permute-start | bytes 589832 | tf_op jit(solution)/shard_map/ppermute | solution.py:12
  132.7 7.1 %collective-permute-start.17 = (bf16[96,1024]{1,0:T(8,128)(2,1)S(1)}, bf16[96,1024]{1,0:T(8,128)(2,1)S(1)}, u32[]{:S(2)}, u32[]{:S(2)}) collective-permute-start(bf16[96,1024]{1,0:T(8,128)(2,1)S(1)} %collective-permute-done.11), channel_id=1, source_target_pairs={{0,4},{4,8},{8,12},{12,16},{16,20},{20,24},{24,28},{28,0},{1,5},{5... | collective-permute-start | bytes 589832 | tf_op jit(solution)/shard_map/ppermute | solution.py:12
  132.7 7.1 %collective-permute-start.14 = (bf16[96,1024]{1,0:T(8,128)(2,1)S(1)}, bf16[96,1024]{1,0:T(8,128)(2,1)S(1)}, u32[]{:S(2)}, u32[]{:S(2)}) collective-permute-start(bf16[96,1024]{1,0:T(8,128)(2,1)S(1)} %collective-permute-done.8), channel_id=1, source_target_pairs={{0,28},{4,0},{8,4},{12,8},{16,12},{20,16},{24,20},{28,24},{1,29},{... | collective-permute-start | bytes 589832 | tf_op jit(solution)/shard_map/ppermute | solution.py:12
  139.8 49.3 %collective-permute-start.23 = (bf16[96,1024]{1,0:T(8,128)(2,1)S(1)}, bf16[96,1024]{1,0:T(8,128)(2,1)S(1)}, u32[]{:S(2)}, u32[]{:S(2)}) collective-permute-start(bf16[96,1024]{1,0:T(8,128)(2,1)S(1)} %collective-permute-done.17), channel_id=1, source_target_pairs={{0,4},{4,8},{8,12},{12,16},{16,20},{20,24},{24,28},{28,0},{1,5},{5... | collective-permute-start | bytes 589832 | tf_op jit(solution)/shard_map/ppermute | solution.py:12
  139.8 50.2 %collective-permute-start.20 = (bf16[96,1024]{1,0:T(8,128)(2,1)S(1)}, bf16[96,1024]{1,0:T(8,128)(2,1)S(1)}, u32[]{:S(2)}, u32[]{:S(2)}) collective-permute-start(bf16[96,1024]{1,0:T(8,128)(2,1)S(1)} %collective-permute-done.14), channel_id=1, source_target_pairs={{0,28},{4,0},{8,4},{12,8},{16,12},{20,16},{24,20},{28,24},{1,29},{... | collective-permute-start | bytes 589832 | tf_op jit(solution)/shard_map/ppermute | solution.py:12
  181.6 3.7 %copy-start.11 = (f32[2,96,96]{2,1,0:T(8,128)S(1)}, f32[2,96,96]{2,1,0:T(8,128)}, u32[]{:S(2)}) copy-start(f32[2,96,96]{2,1,0:T(8,128)} %get-tuple-element.11) | copy-start | bytes 221188
  181.6 3.7 %copy-start.12 = (f32[2,96,96]{2,1,0:T(8,128)S(1)}, f32[2,96,96]{2,1,0:T(8,128)}, u32[]{:S(2)}) copy-start(f32[2,96,96]{2,1,0:T(8,128)} %get-tuple-element.12) | copy-start | bytes 221188
  181.6 4.6 %copy-start.7 = (f32[2,96,96]{2,1,0:T(8,128)S(1)}, f32[2,96,96]{2,1,0:T(8,128)}, u32[]{:S(2)}) copy-start(f32[2,96,96]{2,1,0:T(8,128)} %get-tuple-element.13) | copy-start | bytes 221188
  181.6 4.6 %copy-start.8 = (f32[2,96,96]{2,1,0:T(8,128)S(1)}, f32[2,96,96]{2,1,0:T(8,128)}, u32[]{:S(2)}) copy-start(f32[2,96,96]{2,1,0:T(8,128)} %get-tuple-element.14) | copy-start | bytes 221188
  183.5 3.6 %copy-start.5 = (f32[2,96,96]{2,1,0:T(8,128)S(1)}, f32[2,96,96]{2,1,0:T(8,128)}, u32[]{:S(2)}) copy-start(f32[2,96,96]{2,1,0:T(8,128)} %get-tuple-element.15) | copy-start | bytes 221188
  183.5 3.6 %copy-start.6 = (f32[2,96,96]{2,1,0:T(8,128)S(1)}, f32[2,96,96]{2,1,0:T(8,128)}, u32[]{:S(2)}) copy-start(f32[2,96,96]{2,1,0:T(8,128)} %get-tuple-element.16) | copy-start | bytes 221188
  186.2 1.9 copy-start.3
  186.2 1.9 copy-start.4
  188.1 1.0 copy-start.9
  188.1 1.0 copy-start.10
  188.1 1.9 copy-start.1
  188.1 1.9 copy-start.2
Sparse Core Ops, SparseCore 0:
  118.5 63.0 all-reduce.2
  191.7 55.0 all-gather.1
where the time goes:
time: 267 us
  waiting for transfers between devices  113 us (42%)
  blocking collectives  53.6 us (20%)
  starting transfers between devices  41.6 us (16%)
  matrix products  32.7 us (12%)
  between operations  13.7 us (5%)
  local copies, waits for them, and re-layouts  8.09 us (3%)
  other arithmetic  4.52 us (2%)
    ppermute x24, waiting for transfers between devices, from_behind(): return lax.ppermute(value, axis, pairs)  72.7 us
    all_to_all x1, blocking collectives, on_device(): lax.all_to_all(full_basis, 'pts', split_axis=1, concat_axis=0, tiled=True)  42.4 us
    ppermute x24, starting transfers between devices, from_behind(): return lax.ppermute(value, axis, pairs)  41.5 us
    psum x1, waiting for transfers between devices, pair_block(): g_occ, g_vir = lax.psum((g_occ, g_vir), 'orb')  38.2 us
    all_gather x1, blocking collectives, on_device(): full_basis = lax.all_gather(basis, 'orb', axis=1, tiled=True)  11.2 us
    dot_general x8, matrix products, pair_block(): jnp.einsum('tra,ca->trc', weighted_vir, vir_part, preferred_element_type=...  10.5 us
    dot_general x8, matrix products, pair_block(): jnp.einsum('trc,cq->trq', chi, basis_part, preferred_element_type=jnp.flo...  9.7 us
    dot_general x1, local copies, waits for them, and re-layouts, on_device(): jnp.einsum('rp,trq->ptq', basis_cols, lax.all_gather(projected, 'pts', ax...  7.29 us
  transfers between devices with their start and end apart: 26, of which 10 were waited for; matrix products, arithmetic and copies ran while one was open for 11% of the time, Pallas kernels for 0%

commit v1 on v0

v1 whole, which is shorter than its diff:
```python
import jax
import jax.numpy as jnp
from jax import lax
from jax.sharding import PartitionSpec as P

NOFF = 8


def on_device(phi_occ, phi_vir, eps_occ, eps_vir, taus, pair_mask, basis):
    half = NOFF // 2
    tiles, me = lax.axis_size("pts"), lax.axis_index("pts")
    rows, ntau = phi_occ.shape[0], taus.shape[0]
    expo_occ = jnp.exp(taus[:, None] * eps_occ[None, :])
    expo_vir = jnp.exp(-taus[:, None] * eps_vir[None, :])
    weighted_occ = (phi_occ.astype(jnp.float32)[None] * expo_occ[:, None, :]).astype(jnp.bfloat16)
    weighted_vir = (phi_vir.astype(jnp.float32)[None] * expo_vir[:, None, :]).astype(jnp.bfloat16)
    factors = pair_mask[0].astype(jnp.float32)
    shifts = [k - half if k < half else k - half + 1 for k in range(NOFF)]

    if tiles <= NOFF:
        held = jnp.arange(tiles)
    else:
        held = (me + jnp.arange(-half, half + 1)) % tiles
    mine = (me + jnp.array(shifts)) % tiles
    weight = jnp.sum(jnp.where(held[:, None] == mine[None, :], factors[None, :], 0.0), axis=1)
    weight = jnp.repeat(weight, rows)

    def window(whole):
        if tiles > NOFF:
            whole = jnp.stack(
                [
                    lax.dynamic_index_in_dim(whole, (me + shift) % tiles, 0, False)
                    for shift in range(-half, half + 1)
                ]
            )
        return whole.reshape(-1, whole.shape[-1])

    vir_all = window(lax.all_gather(phi_vir, "pts"))
    occ_all = window(lax.all_gather(phi_occ, "pts"))
    basis_all = window(lax.all_gather(basis, "pts"))
    full_basis = lax.all_gather(basis, "orb", axis=1, tiled=True)
    basis_cols = lax.all_to_all(full_basis, "pts", split_axis=1, concat_axis=0, tiled=True)
    g_occ = jnp.einsum("tro,co->trc", weighted_occ, occ_all, preferred_element_type=jnp.float32)
    g_vir = jnp.einsum("tra,ca->trc", weighted_vir, vir_all, preferred_element_type=jnp.float32)
    both = jnp.stack([g_occ, g_vir])
    both = lax.psum_scatter(both, "orb", scatter_dimension=2, tiled=True)
    chi = (both[0] * both[1] * weight).astype(jnp.bfloat16)
    chi = lax.all_gather(chi, "orb", axis=1, tiled=True)
    projected = jnp.einsum(
        "trc,cq->trq", chi, basis_all, preferred_element_type=jnp.float32
    ).astype(jnp.bfloat16)
    return jnp.einsum(
        "rp,trq->ptq",
        basis_cols,
        lax.all_gather(projected, "pts", axis=1, tiled=True),
        preferred_element_type=jnp.float32,
    )


def solution(mesh):
    placed = (
        P("pts", "orb"),
        P("pts", "orb"),
        P("orb"),
        P("orb"),
        P(),
        P("pts", None),
        P("pts", "orb"),
    )
    return jax.shard_map(
        on_device, mesh=mesh, in_specs=placed, out_specs=P("pts", None, "orb"), check_vma=False
    )
```

time: 267 us -> 229 us (0.86)
  starting transfers between devices: 41.6 us -> 0.15 us
  blocking collectives: 53.6 us -> 80.5 us
  matrix products: 32.7 us -> 14.7 us
  waiting for transfers between devices: 113 us -> 109 us
    all_gather x0 -> x2, waiting for transfers between devices: none -> 79.4 us  [the longest x1 62.8 us: on_device(): vir_all = window(lax.all_gather(phi_vir, 'pts'))]
    ppermute x24 -> x0, waiting for transfers between devices: 72.7 us -> none  [from_behind(): return lax.ppermute(value, axis, pairs)]
    ppermute x24 -> x0, starting transfers between devices: 41.5 us -> none  [from_behind(): return lax.ppermute(value, axis, pairs)]
    psum x1 -> x0, waiting for transfers between devices: 38.2 us -> none  [pair_block(): g_occ, g_vir = lax.psum((g_occ, g_vir), 'orb')]
    all_gather x0 -> x2, blocking collectives: none -> 27.4 us  [the longest x1 18.2 us: on_device(): occ_all = window(lax.all_gather(phi_occ, 'pts'))]
    reduce_scatter x0 -> x1, waiting for transfers between devices: none -> 26.3 us  [on_device(): both = lax.psum_scatter(both, 'orb', scatter_dimension=2, tiled=True)]
    dot_general x24 -> x3, matrix products: 27 us -> 9 us  [the longest x1 5.95 us: on_device(): jnp.einsum('tra,ca->trc', weighted_vir, vir_all, preferred_element_type=j...]
  transfers between devices with their start and end apart: 26 -> 4, of which waited for: 10 -> 4; matrix products, arithmetic and copies ran while one was open for 11% -> 1% of each run, Pallas kernels for 0% -> 0%
where the time goes in v1:
time: 229 us
  waiting for transfers between devices  109 us (48%)
  blocking collectives  80.5 us (35%)
  matrix products  14.7 us (6%)
  between operations  13.3 us (6%)
  local copies, waits for them, and re-layouts  7.54 us (3%)
  other arithmetic  3.79 us (2%)
    all_gather x1, waiting for transfers between devices, on_device(): vir_all = window(lax.all_gather(phi_vir, 'pts'))  62.8 us
    all_to_all x1, blocking collectives, on_device(): lax.all_to_all(full_basis, 'pts', split_axis=1, concat_axis=0, tiled=True)  41 us
    reduce_scatter x1, waiting for transfers between devices, on_device(): both = lax.psum_scatter(both, 'orb', scatter_dimension=2, tiled=True)  26.3 us
    all_gather x1, blocking collectives, on_device(): occ_all = window(lax.all_gather(phi_occ, 'pts'))  18.2 us
    all_gather x1, waiting for transfers between devices, on_device(): basis_all = window(lax.all_gather(basis, 'pts'))  16.5 us
    all_gather x1, blocking collectives, on_device(): full_basis = lax.all_gather(basis, 'orb', axis=1, tiled=True)  12.2 us
    all_gather x1, blocking collectives, on_device(): chi = lax.all_gather(chi, 'orb', axis=1, tiled=True)  9.17 us
    dot_general x1, local copies, waits for them, and re-layouts, on_device(): jnp.einsum('rp,trq->ptq', basis_cols, lax.all_gather(projected, 'pts', ax...  7.29 us
  transfers between devices with their start and end apart: 4, of which 4 were waited for; matrix products, arithmetic and copies ran while one was open for 1% of the time, Pallas kernels for 0%

profile of v1, /device:TPU:0, one launch (start us, length us, event | category | flops | bytes accessed | tf_op | source)
XLA Modules:
  0.0 228.6 jit_solution(2500957558550995210)
XLA Ops:
  6.5 0.0 copy-start.4
  6.5 0.0 copy-start.1
  6.5 0.0 copy-start.3
  6.5 0.0 copy-start.2
  6.5 0.0 all-gather.9.cloned.1.call-start
  6.6 0.7 all-gather.9.cloned.1.call-update
  7.3 0.0 reduce-scatter.2.cloned.1.call-start
  7.3 1.4 convert_element_type.24
  8.7 0.0 copy-done.4
  8.7 0.0 copy-done.1
  8.7 0.0 copy-done.3
  8.8 0.1 multiply_exponential_fusion.1
  8.8 18.2 %all-gather = bf16[768,512]{1,0:T(8,128)(2,1)S(1)} all-gather(bf16[96,512]{1,0:T(8,128)(2,1)S(1)} %copy-done.1), channel_id=2, replica_groups=mesh['pts'=8,'orb'=4] {'pts'}, dimensions={0}, use_global_device_ids=true | all-gather | bytes 884736 | tf_op jit(solution)/shard_map/all_gather | solution.py:39
  27.0 0.4 convolution_bitcast_fusion.1
  27.5 0.0 copy-done.2
  27.5 0.1 multiply_exponential_fusion
  27.6 62.8 %all-gather.9.cloned.1.call-done = bf16[768,5120]{1,0:T(8,128)(2,1)} async-done(((bf16[96,5120]{1,0:T(8,128)(2,1)}), bf16[768,5120]{1,0:T(8,128)(2,1)}) %all-gather.9.cloned.1.call-update) | async-done | bytes 7864336 | tf_op jit(solution)/shard_map/all_gather | solution.py:38
  90.4 6.0 %fusion.6 = f32[1,2,96,768]{3,2,1,0:T(8,128)S(1)} fusion(bf16[768,5120]{1,0:T(8,128)(2,1)} %all-gather.9.cloned.1.call-done, f32[2,5120]{1,0:T(2,128)S(1)} %multiply_exponential_fusion, f32[96,5120]{1,0:T(8,128)S(1)} %convert_element_type.24), kind=kOutput, calls=%fused_computation.8 | convolution fusion | flops 1511915520 | bytes 10461184 | tf_op jit(solution)/shard_map/tra,ca->trc/dot_general | solution.py:44
  96.3 0.0 copy-start.5
  96.3 0.0 copy-start.6
  96.4 0.0 copy-start
  96.4 1.1 pad_maximum_fusion
  97.5 0.0 reduce-scatter.2.cloned.1.call-update
  97.5 0.0 all-gather.11.cloned.1.call-start
  97.5 0.7 all-gather.11.cloned.1.call-update
  98.2 0.0 all-gather.7.cloned.1.call-start
  98.3 0.0 copy-done.5
  98.3 0.0 copy-done.6
  98.3 0.1 select_reduce_fusion
  98.5 0.1 broadcast_in_dim.19
  98.5 0.1 mul.90
  98.6 26.3 %reduce-scatter.2.cloned.1.call-done = f32[2,2,24,768]{3,2,1,0:T(8,128)} async-done(((f32[2,2,96,768]{3,2,1,0:T(8,128)}), f32[2,2,24,768]{3,2,1,0:T(8,128)}) %reduce-scatter.2.cloned.1.call-update) | async-done | bytes 294928 | tf_op jit(solution)/shard_map/reduce_scatter | solution.py:46
  124.9 1.0 fusion.17
  125.9 9.2 %all_gather.31 = bf16[2,96,768]{2,1,0:T(8,128)(2,1)S(1)} all-gather(bf16[2,24,768]{2,1,0:T(8,128)(2,1)S(1)} %fusion.17), channel_id=1, replica_groups=mesh['pts'=8,'orb'=4] {'orb'}, dimensions={1}, use_global_device_ids=true | all-gather | bytes 368640 | tf_op jit(solution)/shard_map/all_gather | solution.py:48
  135.1 16.5 %all-gather.11.cloned.1.call-done = bf16[768,1024]{1,0:T(8,128)(2,1)} async-done(((bf16[96,1024]{1,0:T(8,128)(2,1)}), bf16[768,1024]{1,0:T(8,128)(2,1)}) %all-gather.11.cloned.1.call-update) | async-done | bytes 1572880 | tf_op jit(solution)/shard_map/all_gather | solution.py:40
  151.7 2.6 %fusion.9 = bf16[2,96,1024]{2,1,0:T(8,128)(2,1)} fusion(bf16[2,96,768]{2,1,0:T(8,128)(2,1)S(1)} %all_gather.31, bf16[768,1024]{1,0:T(8,128)(2,1)} %all-gather.11.cloned.1.call-done), kind=kOutput, calls=%fused_computation.9 | convolution fusion | flops 302186496 | bytes 2260992 | tf_op jit(solution)/shard_map/trc,cq->trq/dot_general | solution.py:49
  154.3 0.0 all-gather.7.cloned.1.call-update
  154.3 0.0 copy-done
  154.3 12.2 %all_gather.35 = bf16[96,4096]{1,0:T(8,128)(2,1)S(1)} all-gather(bf16[96,1024]{1,0:T(8,128)(2,1)S(1)} %copy-done), channel_id=1, replica_groups=mesh['pts'=8,'orb'=4] {'orb'}, dimensions={1}, use_global_device_ids=true | all-gather | bytes 983040 | tf_op jit(solution)/shard_map/all_gather | solution.py:41
  166.5 0.1 copy.15
  166.6 41.0 %all_to_all.19 = bf16[96,8,512]{2,0,1:T(8,128)(2,1)S(1)} all-to-all(bf16[96,8,512]{2,0,1:T(8,128)(2,1)S(1)} %bitcast.39), channel_id=1, replica_groups=mesh['pts'=8,'orb'=4] {'pts'}, dimensions={1} | all-to-all | bytes 1572864 | tf_op jit(solution)/shard_map/all_to_all | solution.py:42
  207.6 1.5 all-gather.7.cloned.1.call-done
  209.1 5.7 %convolution_bitcast_fusion = f32[512,2,1024]{0,2,1:T(8,128)} fusion(bf16[2,768,1024]{2,1,0:T(8,128)(2,1)} %all-gather.7.cloned.1.call-done, bf16[768,512,1]{1,0,2:T(8,128)(2,1)S(1)} %bitcast.41), kind=kOutput, calls=%fused_computation.3 | convolution fusion | flops 1610612736 | bytes 8126464 | tf_op jit(solution)/shard_map/rp,trq->ptq/dot_general | solution.py:52
  214.8 7.3 %copy.12 = f32[512,2,1024]{2,1,0:T(2,128)} copy(f32[512,2,1024]{0,2,1:T(8,128)} %convolution_bitcast_fusion) | data formatting | bytes 8388608 | tf_op jit(solution)/shard_map/rp,trq->ptq/dot_general | solution.py:52
  (4 shorter events, 0.0 us)
Async XLA Ops:
  6.5 2.2 copy-start.4
  6.5 2.2 copy-start.1
  6.5 2.2 copy-start.3
  6.5 20.9 %copy-start.2 = (f32[5120]{0:T(1024)S(1)}, f32[5120]{0:T(1024)}, u32[]{:S(2)}) copy-start(f32[5120]{0:T(1024)} %param.11) | copy-start | bytes 61444
  6.5 83.8 %all-gather.9.cloned.1.call-start = ((), (), s32[]{:S(2)}) async-start(), calls=%async_computation.4 | async-start | bytes 8847360 | tf_op jit(solution)/shard_map/all_gather | solution.py:38
  7.3 117.7 %reduce-scatter.2.cloned.1.call-start = ((), (), s32[]{:S(2)}) async-start(), calls=%async_computation.2 | async-start | bytes 1474560 | tf_op jit(solution)/shard_map/reduce_scatter | solution.py:46
  96.3 2.0 copy-start.5
  96.3 2.0 copy-start.6
  96.4 58.0 %copy-start = (bf16[96,1024]{1,0:T(8,128)(2,1)S(1)}, bf16[96,1024]{1,0:T(8,128)(2,1)}, u32[]{:S(2)}) copy-start(bf16[96,1024]{1,0:T(8,128)(2,1)} %param.14) | copy-start | bytes 589828
  97.5 54.2 %all-gather.11.cloned.1.call-start = ((), (), s32[]{:S(2)}) async-start(), calls=%async_computation.5 | async-start | bytes 1769472 | tf_op jit(solution)/shard_map/all_gather | solution.py:40
  98.2 110.9 %all-gather.7.cloned.1.call-start = ((), (), s32[]{:S(2)}) async-start(), calls=%async_computation.3 | async-start | bytes 3538944 | tf_op jit(solution)/shard_map/all_gather | solution.py:55
Sparse Core Ops, SparseCore 0:
  9.0 81.3 all-gather.8
  97.6 27.2 reduce-scatter.1
  126.6 25.0 all-gather.10
  154.4 54.6 all-gather.6

commit v2 on v1

--- a/solution.py
+++ b/solution.py
@@ -1,9 +1,108 @@
+import functools
+
 import jax
 import jax.numpy as jnp
 from jax import lax
+from jax.experimental import pallas as pl
+from jax.experimental.pallas import tpu as pltpu
 from jax.sharding import PartitionSpec as P
 
 NOFF = 8
+
+
+def line_gather_kernel(count, pieces, panel, out, send_sem, recv_sem, own_sem):
+    me = lax.axis_index("pts")
+    place, last = me // 2, count // 2 - 1
+    peer = me + 1 - 2 * (me % 2)
+    high = panel.shape[0] // pieces
+    up, down = place < last, place > 0
+
+    barrier = pltpu.get_barrier_semaphore()
+
+    def greet(target):
+        pl.semaphore_signal(
+            barrier, inc=1, device_id={"pts": target}, device_id_type=pl.DeviceIdType.MESH
+        )
+
+    greet(peer)
+    pl.when(up)(lambda: greet(me + 2))
+    pl.when(down)(lambda: greet(me - 2))
+    pl.semaphore_wait(barrier, 1 + up.astype(jnp.int32) + down.astype(jnp.int32))
+
+    def copy(way, tile, piece, target, own=False):
+        part = pl.ds(piece * high, high)
+        return pltpu.make_async_remote_copy(
+            src_ref=panel.at[part] if own else out.at[tile, part],
+            dst_ref=out.at[tile, part],
+            send_sem=send_sem.at[way, tile, piece],
+            recv_sem=recv_sem.at[tile, piece],
+            device_id={"pts": target},
+            device_id_type=pl.DeviceIdType.MESH,
+        )
+
+    own_copy = pltpu.make_async_copy(panel, out.at[me], own_sem)
+    own_copy.start()
+    for piece in range(pieces):
+        pl.when(up)(lambda: copy(0, me, piece, me + 2, True).start())
+        pl.when(down)(lambda: copy(1, me, piece, me - 2, True).start())
+        copy(2, me, piece, peer, True).start()
+    for step in range(1, last + 1):
+        for piece in range(pieces):
+
+            @pl.when(place >= step)
+            def _():
+                tile = me - 2 * step
+                copy(0, tile, piece, me).wait_recv()
+                pl.when(up)(lambda: copy(0, tile, piece, me + 2).start())
+                copy(2, tile, piece, peer).start()
+
+            @pl.when(place + step <= last)
+            def _():
+                tile = me + 2 * step
+                copy(1, tile, piece, me).wait_recv()
+                pl.when(down)(lambda: copy(1, tile, piece, me - 2).start())
+                copy(2, tile, piece, peer).start()
+
+    for other in range(last + 1):
+        tile = 2 * other + (1 - me % 2)
+        for piece in range(pieces):
+            copy(2, tile, piece, me).wait_recv()
+    own_copy.wait()
+    for piece in range(pieces):
+        pl.when(up)(lambda: copy(0, me, piece, me + 2, True).wait_send())
+        pl.when(down)(lambda: copy(1, me, piece, me - 2, True).wait_send())
+        copy(2, me, piece, peer, True).wait_send()
+    for step in range(1, last + 1):
+        for piece in range(pieces):
+
+            @pl.when(place >= step)
+            def _():
+                tile = me - 2 * step
+                pl.when(up)(lambda: copy(0, tile, piece, me + 2).wait_send())
+                copy(2, tile, piece, peer).wait_send()
+
+            @pl.when(place + step <= last)
+            def _():
+                tile = me + 2 * step
+                pl.when(down)(lambda: copy(1, tile, piece, me - 2).wait_send())
+                copy(2, tile, piece, peer).wait_send()
+
+
+def line_gather(panel, count):
+    rows, width = panel.shape
+    pieces = 3 if rows % 48 == 0 else 1
+    return pl.pallas_call(
+        functools.partial(line_gather_kernel, count, pieces),
+        out_shape=jax.ShapeDtypeStruct((count, rows, width), panel.dtype),
+        in_specs=[pl.BlockSpec(memory_space=pl.ANY)],
+        out_specs=pl.BlockSpec(memory_space=pl.ANY),
+        scratch_shapes=[
+            pltpu.SemaphoreType.DMA((3, count, pieces)),
+            pltpu.SemaphoreType.DMA((count, pieces)),
+            pltpu.SemaphoreType.DMA,
+        ],
+        compiler_params=pltpu.CompilerParams(collective_id=0, has_side_effects=True),
+    )(panel)
 
 
 def on_device(phi_occ, phi_vir, eps_occ, eps_vir, taus, pair_mask, basis):
@@ -35,11 +134,25 @@
             )
         return whole.reshape(-1, whole.shape[-1])
 
-    vir_all = window(lax.all_gather(phi_vir, "pts"))
-    occ_all = window(lax.all_gather(phi_occ, "pts"))
-    basis_all = window(lax.all_gather(basis, "pts"))
-    full_basis = lax.all_gather(basis, "orb", axis=1, tiled=True)
-    basis_cols = lax.all_to_all(full_basis, "pts", split_axis=1, concat_axis=0, tiled=True)
+    if tiles == NOFF:
+        panels = line_gather(jnp.concatenate([phi_vir, phi_occ, basis], axis=1), tiles)
+    else:
+        panels = lax.all_gather(jnp.concatenate([phi_vir, phi_occ, basis], axis=1), "pts")
+    near = window(panels)
+    nvir, nocc = phi_vir.shape[1], phi_occ.shape[1]
+    vir_all, occ_all, basis_all = near[:, :nvir], near[:, nvir : nvir + nocc], near[:, nvir + nocc :]
+    groups = lax.axis_size("orb")
+    if tiles % groups == 0:
+        share = tiles // groups
+        wide = basis.shape[1] // share
+        cols = lax.dynamic_slice_in_dim(
+            panels, nvir + nocc + (me % share) * wide, wide, axis=2
+        ).reshape(tiles * rows, wide)
+        cols = jnp.where(lax.axis_index("orb") == me // share, cols, jnp.zeros_like(cols))
+        basis_cols = lax.psum(cols, "orb")
+    else:
+        full_basis = lax.all_gather(basis, "orb", axis=1, tiled=True)
+        basis_cols = lax.all_to_all(full_basis, "pts", split_axis=1, concat_axis=0, tiled=True)
     g_occ = jnp.einsum("tro,co->trc", weighted_occ, occ_all, preferred_element_type=jnp.float32)
     g_vir = jnp.einsum("tra,ca->trc", weighted_vir, vir_all, preferred_element_type=jnp.float32)
     both = jnp.stack([g_occ, g_vir])

time: 229 us -> 245 us (1.070)
  Pallas kernels: 0 us -> 90.1 us
  blocking collectives: 80.5 us -> 9.18 us
  waiting for transfers between devices: 109 us -> 105 us
  other arithmetic: 3.79 us -> 6.29 us
    pallas_call x0 -> x1, Pallas kernels: none -> 90.1 us  [line_gather(): pl.pallas_call(functools.partial(line_gather_kernel, count, pieces), out_...]
    all_gather x2 -> x0, waiting for transfers between devices: 79.4 us -> none  [the longest x1 62.8 us: on_device(): vir_all = window(lax.all_gather(phi_vir, 'pts'))]
    all_to_all x1 -> x0, blocking collectives: 41 us -> none  [on_device(): lax.all_to_all(full_basis, 'pts', split_axis=1, concat_axis=0, tiled=True)]
    psum x0 -> x1, waiting for transfers between devices: none -> 39 us  [on_device(): basis_cols = lax.psum(cols, 'orb')]
    all_gather x1, waiting for transfers between devices: 1.53 us -> 40 us  [on_device(): lax.all_gather(projected, 'pts', axis=1, tiled=True)]
    all_gather x2 -> x0, blocking collectives: 30.4 us -> none  [the longest x1 18.2 us: on_device(): occ_all = window(lax.all_gather(phi_occ, 'pts'))]
  transfers between devices with their start and end apart: 4 -> 3, of which waited for: 4 -> 3; matrix products, arithmetic and copies ran while one was open for 1% -> 3% of each run, Pallas kernels for 0% -> 0%
where the time goes in v2:
time: 245 us
  waiting for transfers between devices  105 us (43%)
  Pallas kernels  90.1 us (37%)
  matrix products  14.1 us (6%)
  between operations  13.3 us (5%)
  blocking collectives  9.18 us (4%)
  local copies, waits for them, and re-layouts  6.64 us (3%)
  other arithmetic  6.29 us (3%)
    pallas_call x1, Pallas kernels, line_gather(): pl.pallas_call(functools.partial(line_gather_kernel, count, pieces), out_...  90.1 us
    all_gather x1, waiting for transfers between devices, on_device(): lax.all_gather(projected, 'pts', axis=1, tiled=True)  40 us
    psum x1, waiting for transfers between devices, on_device(): basis_cols = lax.psum(cols, 'orb')  39 us
    reduce_scatter x1, waiting for transfers between devices, on_device(): both = lax.psum_scatter(both, 'orb', scatter_dimension=2, tiled=True)  26 us
    all_gather x1, blocking collectives, on_device(): chi = lax.all_gather(chi, 'orb', axis=1, tiled=True)  9.18 us
    dot_general x1, matrix products, on_device(): jnp.einsum('tra,ca->trc', weighted_vir, vir_all, preferred_element_type=j...  5.95 us
    dot_general x1, local copies, waits for them, and re-layouts, on_device(): jnp.einsum('rp,trq->ptq', basis_cols, lax.all_gather(projected, 'pts', ax...  5.25 us
  transfers between devices with their start and end apart: 3, of which 3 were waited for; matrix products, arithmetic and copies ran while one was open for 3% of the time, Pallas kernels for 0%

profile of v2, /device:TPU:0, one launch (start us, length us, event | category | flops | bytes accessed | tf_op | source)
XLA Modules:
  0.0 244.6 jit_solution(15244101833771413052)
XLA Ops:
  6.5 0.0 copy-start
  6.5 0.0 copy-start.1
  6.5 0.0 copy-start.2
  6.5 0.0 reduce-scatter.2.cloned.1.call-start
  6.5 1.5 convert_element_type.24
  8.0 0.0 copy-done.1
  8.0 0.0 copy-done
  8.1 0.0 copy-done.2
  8.1 1.1 pad_maximum_fusion.panel
  9.2 0.0 copy-start.5
  9.2 0.0 copy-start.4
  9.2 0.0 copy-start.3
  9.2 90.1 %shard_map.82 = bf16[8,96,6656]{2,1,0:T(8,128)(2,1)} custom-call(bf16[96,6656]{1,0:T(8,128)(2,1)} %pad_maximum_fusion.panel), custom_call_target="tpu_custom_call" | custom-call | tf_op jit(solution)/shard_map/pallas_call | solution.py:94
  99.4 0.0 copy-done.5
  99.4 0.0 copy-done.4
  99.4 0.1 multiply_exponential_fusion.1
  99.5 0.0 copy-done.3
  99.5 0.1 multiply_exponential_fusion
  99.6 6.0 %fusion.4 = f32[1,2,96,768]{3,2,1,0:T(8,128)S(1)} fusion(bf16[768,6656]{1,0:T(8,128)(2,1)} %bitcast.32, f32[2,5120]{1,0:T(2,128)S(1)} %multiply_exponential_fusion, f32[96,5120]{1,0:T(8,128)S(1)} %convert_element_type.24), kind=kOutput, calls=%fused_computation.8 | convolution fusion | flops 1511915520 | bytes 10461184 | tf_op jit(solution)/shard_map/tra,ca->trc/dot_general | solution.py:157
  105.5 1.5 convolution_bitcast_fusion
  107.1 1.1 pad_maximum_fusion.1
  108.2 0.0 copy-start.7
  108.2 0.0 copy-start.6
  108.2 0.0 reduce-scatter.2.cloned.1.call-update
  108.2 0.0 all-reduce.2.cloned.1.call-start
  108.3 1.3 dynamic-slice_select_fusion
  109.6 1.2 copy.11
  110.7 0.0 all-reduce.2.cloned.1.call-update
  110.8 0.0 all-gather.2.cloned.1.call-start
  110.8 0.0 copy-done.7
  110.8 0.0 copy-done.6
  110.9 0.1 select_reduce_fusion
  111.0 0.1 broadcast_in_dim.35
  111.1 0.1 mul.94
  111.1 26.0 %reduce-scatter.2.cloned.1.call-done = f32[2,2,24,768]{3,2,1,0:T(8,128)} async-done(((f32[2,2,96,768]{3,2,1,0:T(8,128)}), f32[2,2,24,768]{3,2,1,0:T(8,128)}) %reduce-scatter.2.cloned.1.call-update) | async-done | bytes 294928 | tf_op jit(solution)/shard_map/reduce_scatter | solution.py:159
  137.1 1.0 fusion.12
  138.1 9.2 %all_gather.6 = bf16[2,96,768]{2,1,0:T(8,128)(2,1)S(1)} all-gather(bf16[2,24,768]{2,1,0:T(8,128)(2,1)S(1)} %fusion.12), channel_id=1, replica_groups=mesh['pts'=8,'orb'=4] {'orb'}, dimensions={1}, use_global_device_ids=true | all-gather | bytes 368640 | tf_op jit(solution)/shard_map/all_gather | solution.py:161
  147.3 2.6 %fusion.5 = bf16[2,96,1024]{2,1,0:T(8,128)(2,1)} fusion(bf16[2,96,768]{2,1,0:T(8,128)(2,1)S(1)} %all_gather.6, bf16[768,6656]{1,0:T(8,128)(2,1)} %bitcast.34), kind=kOutput, calls=%fused_computation.9 | convolution fusion | flops 302186496 | bytes 2260992 | tf_op jit(solution)/shard_map/trc,cq->trq/dot_general | solution.py:162
  149.9 0.0 all-gather.2.cloned.1.call-update
  149.9 39.0 %all-reduce.2.cloned.1.call-done = bf16[768,512]{0,1:T(8,128)(2,1)} async-done(((bf16[768,512]{0,1:T(8,128)(2,1)}), bf16[768,512]{0,1:T(8,128)(2,1)}) %all-reduce.2.cloned.1.call-update) | async-done | bytes 786448 | tf_op jit(solution)/shard_map/psum | solution.py:152
  188.9 40.0 %all-gather.2.cloned.1.call-done = bf16[2,768,1024]{2,1,0:T(8,128)(2,1)} async-done(((bf16[2,96,1024]{2,1,0:T(8,128)(2,1)}), bf16[2,768,1024]{2,1,0:T(8,128)(2,1)}) %all-gather.2.cloned.1.call-update) | async-done | bytes 3145744 | tf_op jit(solution)/shard_map/all_gather | solution.py:168
  228.9 3.9 %fusion.6 = f32[512,2,1024]{2,0,1:T(8,128)S(1)} fusion(bf16[2,768,1024]{2,1,0:T(8,128)(2,1)} %all-gather.2.cloned.1.call-done, bf16[768,512]{0,1:T(8,128)(2,1)} %all-reduce.2.cloned.1.call-done), kind=kOutput, calls=%fused_computation.13 | convolution fusion | flops 1610612736 | bytes 8126464 | tf_op jit(solution)/shard_map/rp,trq->ptq/dot_general | solution.py:165
  232.9 5.2 %copy.12 = f32[512,2,1024]{2,1,0:T(2,128)} copy(f32[512,2,1024]{2,0,1:T(8,128)S(1)} %fusion.6) | data formatting | bytes 8388608 | tf_op jit(solution)/shard_map/rp,trq->ptq/dot_general | solution.py:165
  (4 shorter events, 0.0 us)
Async XLA Ops:
  6.5 1.5 copy-start
  6.5 1.5 copy-start.1
  6.5 1.6 copy-start.2
  6.5 130.5 %reduce-scatter.2.cloned.1.call-start = ((), (), s32[]{:S(2)}) async-start(), calls=%async_computation.2 | async-start | bytes 1474560 | tf_op jit(solution)/shard_map/reduce_scatter | solution.py:159
  9.2 90.1 %copy-start.5 = (f32[2]{0:T(128)S(1)}, f32[2]{0:T(128)}, u32[]{:S(2)}) copy-start(f32[2]{0:T(128)} %param.12) | copy-start | bytes 28
  9.2 90.2 %copy-start.4 = (f32[512]{0:T(512)S(1)}, f32[512]{0:T(512)}, u32[]{:S(2)}) copy-start(f32[512]{0:T(512)} %param.10) | copy-start | bytes 6148
  9.2 90.2 %copy-start.3 = (f32[5120]{0:T(1024)S(1)}, f32[5120]{0:T(1024)}, u32[]{:S(2)}) copy-start(f32[5120]{0:T(1024)} %param.11) | copy-start | bytes 61444
  108.2 2.6 %copy-start.7 = (s32[8]{0:T(128)S(1)}, s32[8]{0:T(128)}, u32[]{:S(2)}) copy-start(s32[8]{0:T(128)} %constant.61.clone) | copy-start | bytes 100
  108.2 2.7 %copy-start.6 = (s32[1,8]{1,0:T(1,128)S(1)}, s32[1,8]{1,0:T(1,128)}, u32[]{:S(2)}) copy-start(s32[1,8]{1,0:T(1,128)} %param.13) | copy-start | bytes 100
  108.2 80.7 %all-reduce.2.cloned.1.call-start = ((), (), s32[]{:S(2)}) async-start(), calls=%async_computation.1 | async-start | bytes 1572864 | tf_op jit(solution)/shard_map/psum | solution.py:152
  110.8 118.1 %all-gather.2.cloned.1.call-start = ((), (), s32[]{:S(2)}) async-start(), calls=%async_computation.3 | async-start | bytes 3538944 | tf_op jit(solution)/shard_map/all_gather | solution.py:168
Sparse Core Ops, SparseCore 0:
  108.3 28.6 reduce-scatter.1
  140.1 48.7 all-reduce.1
  190.6 38.2 all-gather.1

commit v3 on v2

--- a/solution.py
+++ b/solution.py
@@ -88,7 +88,7 @@
                 copy(2, tile, piece, peer).wait_send()
 
 
-def line_gather(panel, count):
+def line_gather(panel, count, collective_id):
     rows, width = panel.shape
     pieces = 3 if rows % 48 == 0 else 1
     return pl.pallas_call(
@@ -101,7 +101,7 @@
             pltpu.SemaphoreType.DMA((count, pieces)),
             pltpu.SemaphoreType.DMA,
         ],
-        compiler_params=pltpu.CompilerParams(collective_id=0, has_side_effects=True),
+        compiler_params=pltpu.CompilerParams(collective_id=collective_id, has_side_effects=True),
     )(panel)
 
 
@@ -135,7 +135,7 @@
         return whole.reshape(-1, whole.shape[-1])
 
     if tiles == NOFF:
-        panels = line_gather(jnp.concatenate([phi_vir, phi_occ, basis], axis=1), tiles)
+        panels = line_gather(jnp.concatenate([phi_vir, phi_occ, basis], axis=1), tiles, 0)
     else:
         panels = lax.all_gather(jnp.concatenate([phi_vir, phi_occ, basis], axis=1), "pts")
     near = window(panels)
@@ -148,8 +148,17 @@
         cols = lax.dynamic_slice_in_dim(
             panels, nvir + nocc + (me % share) * wide, wide, axis=2
         ).reshape(tiles * rows, wide)
-        cols = jnp.where(lax.axis_index("orb") == me // share, cols, jnp.zeros_like(cols))
-        basis_cols = lax.psum(cols, "orb")
+        here = jnp.where(lax.axis_index("orb") == me // share, cols, jnp.zeros_like(cols))
+        if tiles == NOFF:
+            basis_cols = here
+            for turn in range(1, groups):
+                pairs = [
+                    (tile * groups + tile // share, tile * groups + (tile // share + turn) % groups)
+                    for tile in range(tiles)
+                ]
+                basis_cols = basis_cols + lax.ppermute(cols, ("pts", "orb"), pairs)
+        else:
+            basis_cols = lax.psum(here, "orb")
     else:
         full_basis = lax.all_gather(basis, "orb", axis=1, tiled=True)
         basis_cols = lax.all_to_all(full_basis, "pts", split_axis=1, concat_axis=0, tiled=True)
@@ -162,12 +171,13 @@
     projected = jnp.einsum(
         "trc,cq->trq", chi, basis_all, preferred_element_type=jnp.float32
     ).astype(jnp.bfloat16)
-    return jnp.einsum(
-        "rp,trq->ptq",
-        basis_cols,
-        lax.all_gather(projected, "pts", axis=1, tiled=True),
-        preferred_element_type=jnp.float32,
-    )
+    if tiles == NOFF:
+        flat = line_gather(projected.reshape(ntau * rows, -1), tiles, 1)
+        flat = flat.reshape(tiles, ntau, rows, -1).transpose(1, 0, 2, 3)
+        projected_all = flat.reshape(ntau, tiles * rows, -1)
+    else:
+        projected_all = lax.all_gather(projected, "pts", axis=1, tiled=True)
+    return jnp.einsum("rp,trq->ptq", basis_cols, projected_all, preferred_element_type=jnp.float32)
 
 
 def solution(mesh):

time: 245 us -> 214 us (0.87)
  waiting for transfers between devices: 105 us -> 32.4 us
  Pallas kernels: 90.1 us -> 119 us
  starting transfers between devices: 0.09 us -> 7.08 us
  blocking collectives: 9.18 us -> 13.3 us
    all_gather x1 -> x0, waiting for transfers between devices: 40 us -> none  [on_device(): lax.all_gather(projected, 'pts', axis=1, tiled=True)]
    psum x1 -> x0, waiting for transfers between devices: 39 us -> none  [on_device(): basis_cols = lax.psum(cols, 'orb')]
    pallas_call x1 -> x2, Pallas kernels: 90.1 us -> 119 us  [line_gather(): pl.pallas_call(functools.partial(line_gather_kernel, count, pieces), out_...]
    ppermute x0 -> x3, starting transfers between devices: none -> 7.08 us  [on_device(): basis_cols = basis_cols + lax.ppermute(cols, ('pts', 'orb'), pairs)]
    reduce_scatter x1, waiting for transfers between devices: 26 us -> 32.4 us  [on_device(): both = lax.psum_scatter(both, 'orb', scatter_dimension=2, tiled=True)]
    all_gather x1, blocking collectives: 9.18 us -> 13.3 us  [on_device(): chi = lax.all_gather(chi, 'orb', axis=1, tiled=True)]
  transfers between devices with their start and end apart: 3 -> 4, of which waited for: 3 -> 1; matrix products, arithmetic and copies ran while one was open for 3% -> 3% of each run, Pallas kernels for 0% -> 14%
where the time goes in v3:
time: 214 us
  Pallas kernels  119 us (56%)
  waiting for transfers between devices  32.4 us (15%)
  between operations  13.6 us (6%)
  blocking collectives  13.3 us (6%)
  matrix products  12.1 us (6%)
  local copies, waits for them, and re-layouts  8.94 us (4%)
  other arithmetic  7.25 us (3%)
  starting transfers between devices  7.08 us (3%)
    pallas_call x2, Pallas kernels, line_gather(): pl.pallas_call(functools.partial(line_gather_kernel, count, pieces), out_...  119 us
    reduce_scatter x1, waiting for transfers between devices, on_device(): both = lax.psum_scatter(both, 'orb', scatter_dimension=2, tiled=True)  32.4 us
    all_gather x1, blocking collectives, on_device(): chi = lax.all_gather(chi, 'orb', axis=1, tiled=True)  13.3 us
    ppermute x3, starting transfers between devices, on_device(): basis_cols = basis_cols + lax.ppermute(cols, ('pts', 'orb'), pairs)  7.08 us
    dot_general x1, matrix products, on_device(): jnp.einsum('tra,ca->trc', weighted_vir, vir_all, preferred_element_type=j...  5.96 us
    dot_general x1, local copies, waits for them, and re-layouts, on_device(): jnp.einsum('rp,trq->ptq', basis_cols, projected_all, preferred_element_ty...  5.25 us
  transfers between devices with their start and end apart: 4, of which 1 were waited for; matrix products, arithmetic and copies ran while one was open for 3% of the time, Pallas kernels for 14%

profile of v3, /device:TPU:0, one launch (start us, length us, event | category | flops | bytes accessed | tf_op | source)
XLA Modules:
  0.0 214.0 jit_solution(10389745434827935116)
XLA Ops:
  6.5 0.0 copy-start.1
  6.5 0.0 copy-start
  6.5 0.0 copy-start.2
  6.5 0.0 reduce-scatter.2.cloned.1.call-start
  6.5 0.8 neg.4
  7.3 0.8 multiply_exponential_fusion.1
  8.1 0.9 convert_element_type.22
  9.0 1.4 convert_element_type.24
  10.3 0.0 copy-done.1
  10.4 0.0 copy-done
  10.4 0.0 copy-done.2
  10.4 1.1 pad_maximum_fusion.panel
  11.5 0.0 copy-start.3
  11.5 90.1 %shard_map.82 = bf16[8,96,6656]{2,1,0:T(8,128)(2,1)} custom-call(bf16[96,6656]{1,0:T(8,128)(2,1)} %pad_maximum_fusion.panel), custom_call_target="tpu_custom_call" | custom-call | tf_op jit(solution)/shard_map/pallas_call | solution.py:94
  101.6 0.0 copy-done.3
  101.6 0.1 multiply_exponential_fusion
  101.7 6.0 %fusion.4 = f32[1,2,96,768]{3,2,1,0:T(8,128)S(1)} fusion(bf16[768,6656]{1,0:T(8,128)(2,1)} %bitcast.37, f32[2,5120]{1,0:T(2,128)S(1)} %multiply_exponential_fusion, f32[96,5120]{1,0:T(8,128)S(1)} %convert_element_type.24), kind=kOutput, calls=%fused_computation.8 | convolution fusion | flops 1511915520 | bytes 10461184 | tf_op jit(solution)/shard_map/tra,ca->trc/dot_general | solution.py:166
  107.7 1.5 convolution_bitcast_fusion
  109.3 0.0 copy-start.5
  109.3 0.0 copy-start.4
  109.3 1.1 pad_maximum_fusion.1
  110.4 0.0 reduce-scatter.2.cloned.1.call-update
  110.4 1.2 constant_dynamic-slice_fusion
  111.6 4.4 %collective-permute-start.2 = (bf16[768,512]{1,0:T(8,128)(2,1)S(1)}, bf16[768,512]{1,0:T(8,128)(2,1)S(1)}, u32[]{:S(2)}, u32[]{:S(2)}) collective-permute-start(bf16[768,512]{1,0:T(8,128)(2,1)S(1)} %bitcast.42), channel_id=1, source_target_pairs={{0,3},{4,7},{9,8},{13,12},{18,17},{22,21},{27,26},{31,30}} | collective-permute-start | bytes 2359304 | tf_op jit(solution)/shard_map/ppermute | solution.py:159
  116.1 1.3 collective-permute-start.1
  117.4 1.3 collective-permute-start
  118.7 0.0 copy-done.5
  118.8 0.0 copy-done.4
  118.8 0.1 select_reduce_fusion
  118.9 0.1 broadcast_in_dim.35
  119.0 0.1 mul.94
  119.1 32.4 %reduce-scatter.2.cloned.1.call-done = f32[2,2,24,768]{3,2,1,0:T(8,128)} async-done(((f32[2,2,96,768]{3,2,1,0:T(8,128)}), f32[2,2,24,768]{3,2,1,0:T(8,128)}) %reduce-scatter.2.cloned.1.call-update) | async-done | bytes 294928 | tf_op jit(solution)/shard_map/reduce_scatter | solution.py:168
  151.5 1.0 fusion.18
  152.5 13.3 %all_gather.3 = bf16[2,96,768]{2,1,0:T(8,128)(2,1)S(1)} all-gather(bf16[2,24,768]{2,1,0:T(8,128)(2,1)S(1)} %fusion.18), channel_id=1, replica_groups=mesh['pts'=8,'orb'=4] {'orb'}, dimensions={1}, use_global_device_ids=true | all-gather | bytes 368640 | tf_op jit(solution)/shard_map/all_gather | solution.py:170
  165.8 2.6 %fusion.5 = bf16[2,96,1024]{2,1,0:T(8,128)(2,1)} fusion(bf16[2,96,768]{2,1,0:T(8,128)(2,1)S(1)} %all_gather.3, bf16[768,6656]{1,0:T(8,128)(2,1)} %bitcast.39), kind=kOutput, calls=%fused_computation.9 | convolution fusion | flops 302186496 | bytes 2260992 | tf_op jit(solution)/shard_map/trc,cq->trq/dot_general | solution.py:171
  168.4 29.2 %shard_map.83 = bf16[8,192,1024]{2,1,0:T(8,128)(2,1)} custom-call(bf16[192,1024]{1,0:T(8,128)(2,1)} %bitcast.46), custom_call_target="tpu_custom_call" | custom-call | tf_op jit(solution)/shard_map/pallas_call | solution.py:94
  197.6 2.3 %copy.14 = bf16[2,8,96,1024]{3,2,1,0:T(8,128)(2,1)S(1)} copy(bf16[2,8,96,1024]{3,2,0,1:T(8,128)(2,1)} %bitcast.40) | data formatting | bytes 6291456 | tf_op jit(solution)/shard_map/transpose | solution.py:176
  199.9 0.0 collective-permute-done.2
  199.9 0.0 collective-permute-done.1
  199.9 0.0 collective-permute-done
  199.9 1.9 fusion.6
  201.9 5.2 %copy.16 = f32[512,2,1024]{2,1,0:T(2,128)} copy(f32[512,2,1024]{2,0,1:T(8,128)S(1)} %fusion.6) | data formatting | bytes 8388608 | tf_op jit(solution)/shard_map/rp,trq->ptq/dot_general | solution.py:180
  (2 shorter events, 0.0 us)
Async XLA Ops:
  6.5 3.8 %copy-start.1 = (bf16[96,512]{1,0:T(8,128)(2,1)S(1)}, bf16[96,512]{1,0:T(8,128)(2,1)}, u32[]{:S(2)}) copy-start(bf16[96,512]{1,0:T(8,128)(2,1)} %param.8) | copy-start | bytes 294916
  6.5 3.8 %copy-start = (bf16[96,5120]{1,0:T(8,128)(2,1)S(1)}, bf16[96,5120]{1,0:T(8,128)(2,1)}, u32[]{:S(2)}) copy-start(bf16[96,5120]{1,0:T(8,128)(2,1)} %param.9) | copy-start | bytes 2949124
  6.5 3.8 %copy-start.2 = (bf16[96,1024]{1,0:T(8,128)(2,1)S(1)}, bf16[96,1024]{1,0:T(8,128)(2,1)}, u32[]{:S(2)}) copy-start(bf16[96,1024]{1,0:T(8,128)(2,1)} %param.14) | copy-start | bytes 589828
  6.5 144.9 %reduce-scatter.2.cloned.1.call-start = ((), (), s32[]{:S(2)}) async-start(), calls=%async_computation.1 | async-start | bytes 1474560 | tf_op jit(solution)/shard_map/reduce_scatter | solution.py:168
  11.5 90.1 %copy-start.3 = (f32[5120]{0:T(1024)S(1)}, f32[5120]{0:T(1024)}, u32[]{:S(2)}) copy-start(f32[5120]{0:T(1024)} %param.11) | copy-start | bytes 61444
  109.3 9.5 %copy-start.5 = (s32[8]{0:T(128)S(1)}, s32[8]{0:T(128)}, u32[]{:S(2)}) copy-start(s32[8]{0:T(128)} %constant.61.clone) | copy-start | bytes 100
  109.3 9.5 %copy-start.4 = (s32[1,8]{1,0:T(1,128)S(1)}, s32[1,8]{1,0:T(1,128)}, u32[]{:S(2)}) copy-start(s32[1,8]{1,0:T(1,128)} %param.13) | copy-start | bytes 100
  111.6 88.3 %collective-permute-start.2 = (bf16[768,512]{1,0:T(8,128)(2,1)S(1)}, bf16[768,512]{1,0:T(8,128)(2,1)S(1)}, u32[]{:S(2)}, u32[]{:S(2)}) collective-permute-start(bf16[768,512]{1,0:T(8,128)(2,1)S(1)} %bitcast.42), channel_id=1, source_target_pairs={{0,3},{4,7},{9,8},{13,12},{18,17},{22,21},{27,26},{31,30}} | collective-permute-start | bytes 2359304 | tf_op jit(solution)/shard_map/ppermute | solution.py:159
  116.1 83.9 %collective-permute-start.1 = (bf16[768,512]{1,0:T(8,128)(2,1)S(1)}, bf16[768,512]{1,0:T(8,128)(2,1)S(1)}, u32[]{:S(2)}, u32[]{:S(2)}) collective-permute-start(bf16[768,512]{1,0:T(8,128)(2,1)S(1)} %bitcast.43), channel_id=1, source_target_pairs={{0,2},{4,6},{9,11},{13,15},{18,16},{22,20},{27,25},{31,29}} | collective-permute-start | bytes 2359304 | tf_op jit(solution)/shard_map/ppermute | solution.py:159
  117.4 82.5 %collective-permute-start = (bf16[768,512]{1,0:T(8,128)(2,1)S(1)}, bf16[768,512]{1,0:T(8,128)(2,1)S(1)}, u32[]{:S(2)}, u32[]{:S(2)}) collective-permute-start(bf16[768,512]{1,0:T(8,128)(2,1)S(1)} %bitcast.44), channel_id=1, source_target_pairs={{0,1},{4,5},{9,10},{13,14},{18,19},{22,23},{27,24},{31,28}} | collective-permute-start | bytes 2359304 | tf_op jit(solution)/shard_map/ppermute | solution.py:159
Sparse Core Ops, SparseCore 0:
  110.5 40.8 reduce-scatter.1

commit v4 on v3

--- a/solution.py
+++ b/solution.py
@@ -134,22 +134,31 @@
             )
         return whole.reshape(-1, whole.shape[-1])
 
+    nvir = phi_vir.shape[1]
+    orbitals = jnp.concatenate([phi_vir, phi_occ], axis=1)
+    near = line_gather(orbitals, tiles, 0) if tiles == NOFF else lax.all_gather(orbitals, "pts")
+    near = window(near)
+    vir_all, occ_all = near[:, :nvir], near[:, nvir:]
+    g_occ = jnp.einsum("tro,co->trc", weighted_occ, occ_all, preferred_element_type=jnp.float32)
+    g_vir = jnp.einsum("tra,ca->trc", weighted_vir, vir_all, preferred_element_type=jnp.float32)
+    both = jnp.stack([g_occ, g_vir])
+    both, own_basis = lax.optimization_barrier((both, basis))
+    both = lax.psum_scatter(both, "orb", scatter_dimension=2, tiled=True)
     if tiles == NOFF:
-        panels = line_gather(jnp.concatenate([phi_vir, phi_occ, basis], axis=1), tiles, 0)
+        panels = line_gather(own_basis, tiles, 2)
     else:
-        panels = lax.all_gather(jnp.concatenate([phi_vir, phi_occ, basis], axis=1), "pts")
-    near = window(panels)
-    nvir, nocc = phi_vir.shape[1], phi_occ.shape[1]
-    vir_all, occ_all, basis_all = near[:, :nvir], near[:, nvir : nvir + nocc], near[:, nvir + nocc :]
+        panels = lax.all_gather(own_basis, "pts")
+    basis_all = window(panels)
+    chi = (both[0] * both[1] * weight).astype(jnp.bfloat16)
     groups = lax.axis_size("orb")
     if tiles % groups == 0:
         share = tiles // groups
         wide = basis.shape[1] // share
-        cols = lax.dynamic_slice_in_dim(
-            panels, nvir + nocc + (me % share) * wide, wide, axis=2
-        ).reshape(tiles * rows, wide)
+        cols = lax.dynamic_slice_in_dim(panels, (me % share) * wide, wide, axis=2)
+        cols = cols.reshape(tiles * rows, wide)
         here = jnp.where(lax.axis_index("orb") == me // share, cols, jnp.zeros_like(cols))
         if tiles == NOFF:
+            cols, chi = lax.optimization_barrier((cols, chi))
             basis_cols = here
             for turn in range(1, groups):
                 pairs = [
@@ -162,11 +171,6 @@
     else:
         full_basis = lax.all_gather(basis, "orb", axis=1, tiled=True)
         basis_cols = lax.all_to_all(full_basis, "pts", split_axis=1, concat_axis=0, tiled=True)
-    g_occ = jnp.einsum("tro,co->trc", weighted_occ, occ_all, preferred_element_type=jnp.float32)
-    g_vir = jnp.einsum("tra,ca->trc", weighted_vir, vir_all, preferred_element_type=jnp.float32)
-    both = jnp.stack([g_occ, g_vir])
-    both = lax.psum_scatter(both, "orb", scatter_dimension=2, tiled=True)
-    chi = (both[0] * both[1] * weight).astype(jnp.bfloat16)
     chi = lax.all_gather(chi, "orb", axis=1, tiled=True)
     projected = jnp.einsum(
         "trc,cq->trq", chi, basis_all, preferred_element_type=jnp.float32

time: 214 us -> 217 us (1.014)
  waiting for transfers between devices: 32.4 us -> 8.75 us
  blocking collectives: 13.3 us -> 35.7 us
  Pallas kernels: 119 us -> 125 us
  other arithmetic: 7.25 us -> 4.93 us
    reduce_scatter x1, waiting for transfers between devices: 32.4 us -> 8.73 us  [on_device(): both = lax.psum_scatter(both, 'orb', scatter_dimension=2, tiled=True)]
    all_gather x1, blocking collectives: 13.3 us -> 35.7 us  [on_device(): chi = lax.all_gather(chi, 'orb', axis=1, tiled=True)]
    pallas_call x2 -> x3, Pallas kernels: 119 us -> 125 us  [line_gather(): pl.pallas_call(functools.partial(line_gather_kernel, count, pieces), out_...]
  transfers between devices with their start and end apart: 4 -> 4, of which waited for: 1 -> 1; matrix products, arithmetic and copies ran while one was open for 3% -> 2% of each run, Pallas kernels for 14% -> 22%
where the time goes in v4:
time: 217 us
  Pallas kernels  125 us (58%)
  blocking collectives  35.7 us (16%)
  between operations  13.6 us (6%)
  matrix products  12 us (6%)
  local copies, waits for them, and re-layouts  9.11 us (4%)
  waiting for transfers between devices  8.75 us (4%)
  starting transfers between devices  7.8 us (4%)
  other arithmetic  4.93 us (2%)
    pallas_call x3, Pallas kernels, line_gather(): pl.pallas_call(functools.partial(line_gather_kernel, count, pieces), out_...  125 us
    all_gather x1, blocking collectives, on_device(): chi = lax.all_gather(chi, 'orb', axis=1, tiled=True)  35.7 us
    reduce_scatter x1, waiting for transfers between devices, on_device(): both = lax.psum_scatter(both, 'orb', scatter_dimension=2, tiled=True)  8.73 us
    ppermute x3, starting transfers between devices, on_device(): basis_cols = basis_cols + lax.ppermute(cols, ('pts', 'orb'), pairs)  7.8 us
    dot_general x1, matrix products, on_device(): jnp.einsum('tra,ca->trc', weighted_vir, vir_all, preferred_element_type=j...  5.96 us
    dot_general x1, local copies, waits for them, and re-layouts, on_device(): jnp.einsum('rp,trq->ptq', basis_cols, projected_all, preferred_element_ty...  5.25 us
  transfers between devices with their start and end apart: 4, of which 1 were waited for; matrix products, arithmetic and copies ran while one was open for 2% of the time, Pallas kernels for 22%

profile of v4, /device:TPU:0, one launch (start us, length us, event | category | flops | bytes accessed | tf_op | source)
XLA Modules:
  0.0 216.7 jit_solution(6398317873809702288)
XLA Ops:
  6.5 0.0 copy-start.1
  6.5 0.0 copy-start.2
  6.5 0.0 reduce-scatter.2.cloned.1.call-start
  6.5 1.5 convert_element_type.24
  8.0 0.0 copy-done.1
  8.0 0.0 copy-done.2
  8.0 1.1 pad_maximum_fusion.1.panel
  9.1 0.0 copy-start.5
  9.1 0.0 copy-start.4
  9.1 0.0 copy-start.3
  9.1 77.4 %shard_map.82 = bf16[8,96,5632]{2,1,0:T(8,128)(2,1)} custom-call(bf16[96,5632]{1,0:T(8,128)(2,1)} %pad_maximum_fusion.1.panel), custom_call_target="tpu_custom_call" | custom-call | tf_op jit(solution)/shard_map/pallas_call | solution.py:94
  86.6 0.0 copy-done.5
  86.6 0.0 copy-done.4
  86.6 0.1 multiply_exponential_fusion.1
  86.7 0.0 copy-done.3
  86.7 0.1 multiply_exponential_fusion
  86.8 6.0 %fusion.3 = f32[1,2,96,768]{3,2,1,0:T(8,128)S(1)} fusion(bf16[768,5632]{1,0:T(8,128)(2,1)} %bitcast.37, f32[2,5120]{1,0:T(2,128)S(1)} %multiply_exponential_fusion, f32[96,5120]{1,0:T(8,128)S(1)} %convert_element_type.24), kind=kOutput, calls=%fused_computation.5 | convolution fusion | flops 1511915520 | bytes 10461184 | tf_op jit(solution)/shard_map/tra,ca->trc/dot_general | solution.py:143
  92.8 1.5 convolution_bitcast_fusion
  94.3 1.1 pad_maximum_fusion
  95.4 0.0 copy-start.6
  95.4 0.0 copy-start.7
  95.4 0.0 reduce-scatter.2.cloned.1.call-update
  95.5 18.4 %shard_map.83 = bf16[8,96,1024]{2,1,0:T(8,128)(2,1)} custom-call(bf16[96,1024]{1,0:T(8,128)(2,1)} %panel), custom_call_target="tpu_custom_call" | custom-call | tf_op jit(solution)/shard_map/pallas_call | solution.py:94
  113.9 0.0 copy-start
  113.9 0.0 copy-done.6
  114.0 0.0 copy-done.7
  114.0 0.1 select_reduce_fusion
  114.1 0.1 broadcast_in_dim.35
  114.2 0.1 mul.94
  114.2 1.3 constant_dynamic-slice_fusion
  115.6 8.7 %reduce-scatter.2.cloned.1.call-done = f32[2,2,24,768]{3,2,1,0:T(8,128)} async-done(((f32[2,2,96,768]{3,2,1,0:T(8,128)}), f32[2,2,24,768]{3,2,1,0:T(8,128)}) %reduce-scatter.2.cloned.1.call-update) | async-done | bytes 294928 | tf_op jit(solution)/shard_map/reduce_scatter | solution.py:146
  124.3 1.0 fusion.16
  125.3 3.4 %collective-permute-start.2 = (bf16[768,512]{1,0:T(8,128)(2,1)S(1)}, bf16[768,512]{1,0:T(8,128)(2,1)S(1)}, u32[]{:S(2)}, u32[]{:S(2)}) collective-permute-start(bf16[768,512]{1,0:T(8,128)(2,1)S(1)} %bitcast.42), channel_id=1, source_target_pairs={{0,3},{4,7},{9,8},{13,12},{18,17},{22,21},{27,26},{31,30}} | collective-permute-start | bytes 2359304 | tf_op jit(solution)/shard_map/ppermute | solution.py:168
  128.7 2.2 %collective-permute-start.1 = (bf16[768,512]{1,0:T(8,128)(2,1)S(1)}, bf16[768,512]{1,0:T(8,128)(2,1)}, u32[]{:S(2)}, u32[]{:S(2)}) collective-permute-start(bf16[768,512]{1,0:T(8,128)(2,1)S(1)} %bitcast.43), channel_id=1, source_target_pairs={{0,2},{4,6},{9,11},{13,15},{18,16},{22,20},{27,25},{31,29}} | collective-permute-start | bytes 2359304 | tf_op jit(solution)/shard_map/ppermute | solution.py:168
  130.9 2.2 %collective-permute-start = (bf16[768,512]{1,0:T(8,128)(2,1)S(1)}, bf16[768,512]{1,0:T(8,128)(2,1)}, u32[]{:S(2)}, u32[]{:S(2)}) collective-permute-start(bf16[768,512]{1,0:T(8,128)(2,1)S(1)} %bitcast.44), channel_id=1, source_target_pairs={{0,1},{4,5},{9,10},{13,14},{18,19},{22,23},{27,24},{31,28}} | collective-permute-start | bytes 2359304 | tf_op jit(solution)/shard_map/ppermute | solution.py:168
  133.1 35.7 %all_gather.3 = bf16[2,96,768]{2,1,0:T(8,128)(2,1)S(1)} all-gather(bf16[2,24,768]{2,1,0:T(8,128)(2,1)S(1)} %fusion.16), channel_id=1, replica_groups=mesh['pts'=8,'orb'=4] {'orb'}, dimensions={1}, use_global_device_ids=true | all-gather | bytes 368640 | tf_op jit(solution)/shard_map/all_gather | solution.py:174
  168.8 0.0 copy-done
  168.8 1.2 convolution_convert_fusion
  170.1 28.8 %shard_map.84 = bf16[8,192,1024]{2,1,0:T(8,128)(2,1)} custom-call(bf16[192,1024]{1,0:T(8,128)(2,1)} %bitcast.41), custom_call_target="tpu_custom_call" | custom-call | tf_op jit(solution)/shard_map/pallas_call | solution.py:94
  198.9 2.3 %copy.14 = bf16[2,8,96,1024]{3,2,1,0:T(8,128)(2,1)S(1)} copy(bf16[2,8,96,1024]{3,2,0,1:T(8,128)(2,1)} %bitcast.36) | data formatting | bytes 6291456 | tf_op jit(solution)/shard_map/transpose | solution.py:180
  201.2 0.0 collective-permute-done.2
  201.2 0.0 collective-permute-done.1
  201.2 0.0 collective-permute-done
  201.2 3.3 %fusion.4 = f32[512,2,1024]{2,0,1:T(8,128)S(1)} fusion(bf16[2,768,1024]{2,1,0:T(8,128)(2,1)S(1)} %bitcast.40, bf16[768,512]{1,0:T(8,128)(2,1)S(1)} %collective-permute-done.2, bf16[768,512]{1,0:T(8,128)(2,1)} %collective-permute-done.1, bf16[768,512]{1,0:T(8,128)(2,1)} %collective-permute-done, bf16[768,512]{1,0:T(8,128)(2,1)S(1)} %bitcast.45, pred[]{:T(512)S(6)} %eq.20), kind=kOutput, calls=%fused_computation.11 | convolution fusion | flops 1614151680 | bytes 10485761 | tf_op jit(solution)/shard_map/rp,trq->ptq/dot_general | solution.py:184
  204.6 5.2 %copy.16 = f32[512,2,1024]{2,1,0:T(2,128)} copy(f32[512,2,1024]{2,0,1:T(8,128)S(1)} %fusion.4) | data formatting | bytes 8388608 | tf_op jit(solution)/shard_map/rp,trq->ptq/dot_general | solution.py:184
  (4 shorter events, 0.0 us)
Async XLA Ops:
  6.5 1.5 copy-start.1
  6.5 1.5 copy-start.2
  6.5 117.8 %reduce-scatter.2.cloned.1.call-start = ((), (), s32[]{:S(2)}) async-start(), calls=%async_computation.1 | async-start | bytes 1474560 | tf_op jit(solution)/shard_map/reduce_scatter | solution.py:146
  9.1 77.5 %copy-start.5 = (f32[2]{0:T(128)S(1)}, f32[2]{0:T(128)}, u32[]{:S(2)}) copy-start(f32[2]{0:T(128)} %param.12) | copy-start | bytes 28
  9.1 77.5 %copy-start.4 = (f32[512]{0:T(512)S(1)}, f32[512]{0:T(512)}, u32[]{:S(2)}) copy-start(f32[512]{0:T(512)} %param.10) | copy-start | bytes 6148
  9.1 77.6 %copy-start.3 = (f32[5120]{0:T(1024)S(1)}, f32[5120]{0:T(1024)}, u32[]{:S(2)}) copy-start(f32[5120]{0:T(1024)} %param.11) | copy-start | bytes 61444
  95.4 18.5 %copy-start.6 = (s32[1,8]{1,0:T(1,128)S(1)}, s32[1,8]{1,0:T(1,128)}, u32[]{:S(2)}) copy-start(s32[1,8]{1,0:T(1,128)} %param.13) | copy-start | bytes 100
  95.4 18.5 %copy-start.7 = (s32[8]{0:T(128)S(1)}, s32[8]{0:T(128)}, u32[]{:S(2)}) copy-start(s32[8]{0:T(128)} %constant.58.clone) | copy-start | bytes 100
  113.9 54.9 %copy-start = (bf16[8,96,1024]{2,1,0:T(8,128)(2,1)S(1)}, bf16[8,96,1024]{2,1,0:T(8,128)(2,1)}, u32[]{:S(2)}) copy-start(bf16[8,96,1024]{2,1,0:T(8,128)(2,1)} %shard_map.83) | copy-start | bytes 4718596
  125.3 75.9 %collective-permute-start.2 = (bf16[768,512]{1,0:T(8,128)(2,1)S(1)}, bf16[768,512]{1,0:T(8,128)(2,1)S(1)}, u32[]{:S(2)}, u32[]{:S(2)}) collective-permute-start(bf16[768,512]{1,0:T(8,128)(2,1)S(1)} %bitcast.42), channel_id=1, source_target_pairs={{0,3},{4,7},{9,8},{13,12},{18,17},{22,21},{27,26},{31,30}} | collective-permute-start | bytes 2359304 | tf_op jit(solution)/shard_map/ppermute | solution.py:168
  128.7 72.5 %collective-permute-start.1 = (bf16[768,512]{1,0:T(8,128)(2,1)S(1)}, bf16[768,512]{1,0:T(8,128)(2,1)}, u32[]{:S(2)}, u32[]{:S(2)}) collective-permute-start(bf16[768,512]{1,0:T(8,128)(2,1)S(1)} %bitcast.43), channel_id=1, source_target_pairs={{0,2},{4,6},{9,11},{13,15},{18,16},{22,20},{27,25},{31,29}} | collective-permute-start | bytes 2359304 | tf_op jit(solution)/shard_map/ppermute | solution.py:168
  130.9 70.3 %collective-permute-start = (bf16[768,512]{1,0:T(8,128)(2,1)S(1)}, bf16[768,512]{1,0:T(8,128)(2,1)}, u32[]{:S(2)}, u32[]{:S(2)}) collective-permute-start(bf16[768,512]{1,0:T(8,128)(2,1)S(1)} %bitcast.44), channel_id=1, source_target_pairs={{0,1},{4,5},{9,10},{13,14},{18,19},{22,23},{27,24},{31,28}} | collective-permute-start | bytes 2359304 | tf_op jit(solution)/shard_map/ppermute | solution.py:168
Sparse Core Ops, SparseCore 0:
  95.6 28.6 reduce-scatter.1

commit v5 on v4

--- a/solution.py
+++ b/solution.py
@@ -150,6 +150,7 @@
         panels = lax.all_gather(own_basis, "pts")
     basis_all = window(panels)
     chi = (both[0] * both[1] * weight).astype(jnp.bfloat16)
+    chi = lax.all_gather(chi, "orb", axis=1, tiled=True)
     groups = lax.axis_size("orb")
     if tiles % groups == 0:
         share = tiles // groups
@@ -171,7 +172,6 @@
     else:
         full_basis = lax.all_gather(basis, "orb", axis=1, tiled=True)
         basis_cols = lax.all_to_all(full_basis, "pts", split_axis=1, concat_axis=0, tiled=True)
-    chi = lax.all_gather(chi, "orb", axis=1, tiled=True)
     projected = jnp.einsum(
         "trc,cq->trq", chi, basis_all, preferred_element_type=jnp.float32
     ).astype(jnp.bfloat16)

time: 217 us -> 191 us (0.88)
  blocking collectives: 35.7 us -> 9.18 us
    all_gather x1, blocking collectives: 35.7 us -> 9.18 us  [on_device(): chi = lax.all_gather(chi, 'orb', axis=1, tiled=True)]
  transfers between devices with their start and end apart: 4 -> 4, of which waited for: 1 -> 1; matrix products, arithmetic and copies ran while one was open for 2% -> 3% of each run, Pallas kernels for 22% -> 25%
where the time goes in v5:
time: 191 us; the launch traced here: 189 us
  Pallas kernels  124 us (65%)
  between operations  13.6 us (7%)
  matrix products  12 us (6%)
  blocking collectives  9.18 us (5%)
  local copies, waits for them, and re-layouts  9.11 us (5%)
  waiting for transfers between devices  8.75 us (5%)
  starting transfers between devices  7.79 us (4%)
  other arithmetic  4.93 us (3%)
    pallas_call x3, Pallas kernels, line_gather(): pl.pallas_call(functools.partial(line_gather_kernel, count, pieces), out_...  124 us
    all_gather x1, blocking collectives, on_device(): chi = lax.all_gather(chi, 'orb', axis=1, tiled=True)  9.18 us
    reduce_scatter x1, waiting for transfers between devices, on_device(): both = lax.psum_scatter(both, 'orb', scatter_dimension=2, tiled=True)  8.73 us
    ppermute x3, starting transfers between devices, on_device(): basis_cols = basis_cols + lax.ppermute(cols, ('pts', 'orb'), pairs)  7.79 us
    dot_general x1, matrix products, on_device(): jnp.einsum('tra,ca->trc', weighted_vir, vir_all, preferred_element_type=j...  5.96 us
    dot_general x1, local copies, waits for them, and re-layouts, on_device(): jnp.einsum('rp,trq->ptq', basis_cols, projected_all, preferred_element_ty...  5.25 us
  transfers between devices with their start and end apart: 4, of which 1 were waited for; matrix products, arithmetic and copies ran while one was open for 3% of the time, Pallas kernels for 25%

profile of v5, /device:TPU:0, one launch (start us, length us, event | category | flops | bytes accessed | tf_op | source)
XLA Modules:
  0.0 189.3 jit_solution(2964259378114014321)
XLA Ops:
  6.5 0.0 copy-start.1
  6.5 0.0 copy-start.2
  6.5 0.0 reduce-scatter.2.cloned.1.call-start
  6.5 1.5 convert_element_type.24
  8.0 0.0 copy-done.1
  8.0 0.0 copy-done.2
  8.0 1.1 pad_maximum_fusion.1.panel
  9.1 0.0 copy-start.5
  9.1 0.0 copy-start.4
  9.1 0.0 copy-start.3
  9.1 77.4 %shard_map.82 = bf16[8,96,5632]{2,1,0:T(8,128)(2,1)} custom-call(bf16[96,5632]{1,0:T(8,128)(2,1)} %pad_maximum_fusion.1.panel), custom_call_target="tpu_custom_call" | custom-call | tf_op jit(solution)/shard_map/pallas_call | solution.py:94
  86.6 0.0 copy-done.5
  86.6 0.0 copy-done.4
  86.6 0.1 multiply_exponential_fusion.1
  86.7 0.0 copy-done.3
  86.7 0.1 multiply_exponential_fusion
  86.8 6.0 %fusion.3 = f32[1,2,96,768]{3,2,1,0:T(8,128)S(1)} fusion(bf16[768,5632]{1,0:T(8,128)(2,1)} %bitcast.37, f32[2,5120]{1,0:T(2,128)S(1)} %multiply_exponential_fusion, f32[96,5120]{1,0:T(8,128)S(1)} %convert_element_type.24), kind=kOutput, calls=%fused_computation.5 | convolution fusion | flops 1511915520 | bytes 10461184 | tf_op jit(solution)/shard_map/tra,ca->trc/dot_general | solution.py:143
  92.8 1.5 convolution_bitcast_fusion
  94.3 1.1 pad_maximum_fusion
  95.4 0.0 copy-start.6
  95.4 0.0 copy-start.7
  95.4 0.0 reduce-scatter.2.cloned.1.call-update
  95.5 18.4 %shard_map.83 = bf16[8,96,1024]{2,1,0:T(8,128)(2,1)} custom-call(bf16[96,1024]{1,0:T(8,128)(2,1)} %panel), custom_call_target="tpu_custom_call" | custom-call | tf_op jit(solution)/shard_map/pallas_call | solution.py:94
  113.9 0.0 copy-start
  113.9 0.0 copy-done.6
  114.0 0.0 copy-done.7
  114.0 0.1 select_reduce_fusion
  114.1 0.1 broadcast_in_dim.35
  114.2 0.1 mul.94
  114.2 1.3 constant_dynamic-slice_fusion
  115.6 8.7 %reduce-scatter.2.cloned.1.call-done = f32[2,2,24,768]{3,2,1,0:T(8,128)} async-done(((f32[2,2,96,768]{3,2,1,0:T(8,128)}), f32[2,2,24,768]{3,2,1,0:T(8,128)}) %reduce-scatter.2.cloned.1.call-update) | async-done | bytes 294928 | tf_op jit(solution)/shard_map/reduce_scatter | solution.py:146
  124.3 1.0 fusion.16
  125.3 9.2 %all_gather.3 = bf16[2,96,768]{2,1,0:T(8,128)(2,1)S(1)} all-gather(bf16[2,24,768]{2,1,0:T(8,128)(2,1)S(1)} %fusion.16), channel_id=1, replica_groups=mesh['pts'=8,'orb'=4] {'orb'}, dimensions={1}, use_global_device_ids=true | all-gather | bytes 368640 | tf_op jit(solution)/shard_map/all_gather | solution.py:153
  134.5 3.4 %collective-permute-start.2 = (bf16[768,512]{1,0:T(8,128)(2,1)S(1)}, bf16[768,512]{1,0:T(8,128)(2,1)S(1)}, u32[]{:S(2)}, u32[]{:S(2)}) collective-permute-start(bf16[768,512]{1,0:T(8,128)(2,1)S(1)} %bitcast.42), channel_id=1, source_target_pairs={{0,3},{4,7},{9,8},{13,12},{18,17},{22,21},{27,26},{31,30}} | collective-permute-start | bytes 2359304 | tf_op jit(solution)/shard_map/ppermute | solution.py:169
  137.9 2.2 %collective-permute-start.1 = (bf16[768,512]{1,0:T(8,128)(2,1)S(1)}, bf16[768,512]{1,0:T(8,128)(2,1)}, u32[]{:S(2)}, u32[]{:S(2)}) collective-permute-start(bf16[768,512]{1,0:T(8,128)(2,1)S(1)} %bitcast.43), channel_id=1, source_target_pairs={{0,2},{4,6},{9,11},{13,15},{18,16},{22,20},{27,25},{31,29}} | collective-permute-start | bytes 2359304 | tf_op jit(solution)/shard_map/ppermute | solution.py:169
  140.1 2.2 %collective-permute-start = (bf16[768,512]{1,0:T(8,128)(2,1)S(1)}, bf16[768,512]{1,0:T(8,128)(2,1)}, u32[]{:S(2)}, u32[]{:S(2)}) collective-permute-start(bf16[768,512]{1,0:T(8,128)(2,1)S(1)} %bitcast.44), channel_id=1, source_target_pairs={{0,1},{4,5},{9,10},{13,14},{18,19},{22,23},{27,24},{31,28}} | collective-permute-start | bytes 2359304 | tf_op jit(solution)/shard_map/ppermute | solution.py:169
  142.3 0.0 copy-done
  142.3 1.2 convolution_convert_fusion
  143.5 28.0 %shard_map.84 = bf16[8,192,1024]{2,1,0:T(8,128)(2,1)} custom-call(bf16[192,1024]{1,0:T(8,128)(2,1)} %bitcast.41), custom_call_target="tpu_custom_call" | custom-call | tf_op jit(solution)/shard_map/pallas_call | solution.py:94
  171.5 2.3 %copy.14 = bf16[2,8,96,1024]{3,2,1,0:T(8,128)(2,1)S(1)} copy(bf16[2,8,96,1024]{3,2,0,1:T(8,128)(2,1)} %bitcast.36) | data formatting | bytes 6291456 | tf_op jit(solution)/shard_map/transpose | solution.py:180
  173.8 0.0 collective-permute-done.2
  173.8 0.0 collective-permute-done.1
  173.8 0.0 collective-permute-done
  173.8 3.3 %fusion.4 = f32[512,2,1024]{2,0,1:T(8,128)S(1)} fusion(bf16[2,768,1024]{2,1,0:T(8,128)(2,1)S(1)} %bitcast.40, bf16[768,512]{1,0:T(8,128)(2,1)S(1)} %collective-permute-done.2, bf16[768,512]{1,0:T(8,128)(2,1)} %collective-permute-done.1, bf16[768,512]{1,0:T(8,128)(2,1)} %collective-permute-done, bf16[768,512]{1,0:T(8,128)(2,1)S(1)} %bitcast.45, pred[]{:T(512)S(6)} %eq.20), kind=kOutput, calls=%fused_computation.11 | convolution fusion | flops 1614151680 | bytes 10485761 | tf_op jit(solution)/shard_map/rp,trq->ptq/dot_general | solution.py:184
  177.2 5.2 %copy.16 = f32[512,2,1024]{2,1,0:T(2,128)} copy(f32[512,2,1024]{2,0,1:T(8,128)S(1)} %fusion.4) | data formatting | bytes 8388608 | tf_op jit(solution)/shard_map/rp,trq->ptq/dot_general | solution.py:184
  (4 shorter events, 0.0 us)
Async XLA Ops:
  6.5 1.5 copy-start.1
  6.5 1.5 copy-start.2
  6.5 117.8 %reduce-scatter.2.cloned.1.call-start = ((), (), s32[]{:S(2)}) async-start(), calls=%async_computation.1 | async-start | bytes 1474560 | tf_op jit(solution)/shard_map/reduce_scatter | solution.py:146
  9.1 77.5 %copy-start.5 = (f32[2]{0:T(128)S(1)}, f32[2]{0:T(128)}, u32[]{:S(2)}) copy-start(f32[2]{0:T(128)} %param.12) | copy-start | bytes 28
  9.1 77.5 %copy-start.4 = (f32[512]{0:T(512)S(1)}, f32[512]{0:T(512)}, u32[]{:S(2)}) copy-start(f32[512]{0:T(512)} %param.10) | copy-start | bytes 6148
  9.1 77.6 %copy-start.3 = (f32[5120]{0:T(1024)S(1)}, f32[5120]{0:T(1024)}, u32[]{:S(2)}) copy-start(f32[5120]{0:T(1024)} %param.11) | copy-start | bytes 61444
  95.4 18.5 %copy-start.6 = (s32[1,8]{1,0:T(1,128)S(1)}, s32[1,8]{1,0:T(1,128)}, u32[]{:S(2)}) copy-start(s32[1,8]{1,0:T(1,128)} %param.13) | copy-start | bytes 100
  95.4 18.5 %copy-start.7 = (s32[8]{0:T(128)S(1)}, s32[8]{0:T(128)}, u32[]{:S(2)}) copy-start(s32[8]{0:T(128)} %constant.58.clone) | copy-start | bytes 100
  113.9 28.4 %copy-start = (bf16[8,96,1024]{2,1,0:T(8,128)(2,1)S(1)}, bf16[8,96,1024]{2,1,0:T(8,128)(2,1)}, u32[]{:S(2)}) copy-start(bf16[8,96,1024]{2,1,0:T(8,128)(2,1)} %shard_map.83) | copy-start | bytes 4718596
  134.5 39.3 %collective-permute-start.2 = (bf16[768,512]{1,0:T(8,128)(2,1)S(1)}, bf16[768,512]{1,0:T(8,128)(2,1)S(1)}, u32[]{:S(2)}, u32[]{:S(2)}) collective-permute-start(bf16[768,512]{1,0:T(8,128)(2,1)S(1)} %bitcast.42), channel_id=1, source_target_pairs={{0,3},{4,7},{9,8},{13,12},{18,17},{22,21},{27,26},{31,30}} | collective-permute-start | bytes 2359304 | tf_op jit(solution)/shard_map/ppermute | solution.py:169
  137.9 35.9 %collective-permute-start.1 = (bf16[768,512]{1,0:T(8,128)(2,1)S(1)}, bf16[768,512]{1,0:T(8,128)(2,1)}, u32[]{:S(2)}, u32[]{:S(2)}) collective-permute-start(bf16[768,512]{1,0:T(8,128)(2,1)S(1)} %bitcast.43), channel_id=1, source_target_pairs={{0,2},{4,6},{9,11},{13,15},{18,16},{22,20},{27,25},{31,29}} | collective-permute-start | bytes 2359304 | tf_op jit(solution)/shard_map/ppermute | solution.py:169
  140.1 33.7 %collective-permute-start = (bf16[768,512]{1,0:T(8,128)(2,1)S(1)}, bf16[768,512]{1,0:T(8,128)(2,1)}, u32[]{:S(2)}, u32[]{:S(2)}) collective-permute-start(bf16[768,512]{1,0:T(8,128)(2,1)S(1)} %bitcast.44), channel_id=1, source_target_pairs={{0,1},{4,5},{9,10},{13,14},{18,19},{22,23},{27,24},{31,28}} | collective-permute-start | bytes 2359304 | tf_op jit(solution)/shard_map/ppermute | solution.py:169
Sparse Core Ops, SparseCore 0:
  95.6 28.6 reduce-scatter.1

commit v6 on v5

--- a/solution.py
+++ b/solution.py
@@ -134,22 +134,22 @@
             )
         return whole.reshape(-1, whole.shape[-1])
 
-    nvir = phi_vir.shape[1]
-    orbitals = jnp.concatenate([phi_vir, phi_occ], axis=1)
-    near = line_gather(orbitals, tiles, 0) if tiles == NOFF else lax.all_gather(orbitals, "pts")
-    near = window(near)
-    vir_all, occ_all = near[:, :nvir], near[:, nvir:]
+    def gather(panel, collective_id):
+        if tiles == NOFF:
+            return line_gather(panel, tiles, collective_id)
+        return lax.all_gather(panel, "pts")
+
+    occ_all = window(gather(phi_occ, 0))
     g_occ = jnp.einsum("tro,co->trc", weighted_occ, occ_all, preferred_element_type=jnp.float32)
+    g_occ, own_vir = lax.optimization_barrier((g_occ, phi_vir))
+    sum_occ = lax.psum_scatter(g_occ, "orb", scatter_dimension=1, tiled=True)
+    vir_all = window(gather(own_vir, 3))
     g_vir = jnp.einsum("tra,ca->trc", weighted_vir, vir_all, preferred_element_type=jnp.float32)
-    both = jnp.stack([g_occ, g_vir])
-    both, own_basis = lax.optimization_barrier((both, basis))
-    both = lax.psum_scatter(both, "orb", scatter_dimension=2, tiled=True)
-    if tiles == NOFF:
-        panels = line_gather(own_basis, tiles, 2)
-    else:
-        panels = lax.all_gather(own_basis, "pts")
+    g_vir, own_basis = lax.optimization_barrier((g_vir, basis))
+    sum_vir = lax.psum_scatter(g_vir, "orb", scatter_dimension=1, tiled=True)
+    panels = gather(own_basis, 2)
     basis_all = window(panels)
-    chi = (both[0] * both[1] * weight).astype(jnp.bfloat16)
+    chi = (sum_occ * sum_vir * weight).astype(jnp.bfloat16)
     chi = lax.all_gather(chi, "orb", axis=1, tiled=True)
     groups = lax.axis_size("orb")
     if tiles % groups == 0:

time: 191 us -> 194 us (1.016)
  Pallas kernels: 124 us -> 131 us
  waiting for transfers between devices: 8.75 us -> 4.96 us
    pallas_call x3 -> x4, Pallas kernels: 124 us -> 131 us  [line_gather(): pl.pallas_call(functools.partial(line_gather_kernel, count, pieces), out_...]
    reduce_scatter x1 -> x2, waiting for transfers between devices: 8.73 us -> 4.92 us  [the longest x1 4.9 us: on_device(): sum_vir = lax.psum_scatter(g_vir, 'orb', scatter_dimension=1, tiled=True)]
  transfers between devices with their start and end apart: 4 -> 5, of which waited for: 1 -> 1; matrix products, arithmetic and copies ran while one was open for 3% -> 6% of each run, Pallas kernels for 25% -> 60%
where the time goes in v6:
time: 194 us; the launch traced here: 193 us
  Pallas kernels  131 us (68%)
  matrix products  13.8 us (7%)
  between operations  13.6 us (7%)
  blocking collectives  9.18 us (5%)
  local copies, waits for them, and re-layouts  9.05 us (5%)
  starting transfers between devices  7.81 us (4%)
  waiting for transfers between devices  4.96 us (3%)
  other arithmetic  3.16 us (2%)
    pallas_call x4, Pallas kernels, line_gather(): pl.pallas_call(functools.partial(line_gather_kernel, count, pieces), out_...  131 us
    all_gather x1, blocking collectives, on_device(): chi = lax.all_gather(chi, 'orb', axis=1, tiled=True)  9.18 us
    ppermute x3, starting transfers between devices, on_device(): basis_cols = basis_cols + lax.ppermute(cols, ('pts', 'orb'), pairs)  7.77 us
    dot_general x1, matrix products, on_device(): jnp.einsum('tra,ca->trc', weighted_vir, vir_all, preferred_element_type=j...  6.84 us
    dot_general x1, local copies, waits for them, and re-layouts, on_device(): jnp.einsum('rp,trq->ptq', basis_cols, projected_all, preferred_element_ty...  5.25 us
    reduce_scatter x1, waiting for transfers between devices, on_device(): sum_vir = lax.psum_scatter(g_vir, 'orb', scatter_dimension=1, tiled=True)  4.9 us
  transfers between devices with their start and end apart: 5, of which 1 were waited for; matrix products, arithmetic and copies ran while one was open for 6% of the time, Pallas kernels for 60%

profile of v6, /device:TPU:0, one launch (start us, length us, event | category | flops | bytes accessed | tf_op | source)
XLA Modules:
  0.0 193.0 jit_solution(7361438754982547162)
XLA Ops:
  6.5 0.0 copy-start.3
  6.5 0.0 copy-start.1
  6.5 0.0 copy-start.2
  6.5 0.0 reduce-scatter.3.cloned.1.call-start
  6.5 1.0 convert_element_type.24
  7.6 16.5 %shard_map.82 = bf16[8,96,512]{2,1,0:T(8,128)(2,1)} custom-call(bf16[96,512]{1,0:T(8,128)(2,1)} %panel.1), custom_call_target="tpu_custom_call" | custom-call | tf_op jit(solution)/shard_map/pallas_call | solution.py:94
  24.0 0.8 multiply_exponential_fusion.1
  24.8 2.4 %fusion.11 = f32[2,96,768]{2,1,0:T(8,128)} fusion(bf16[768,512,1]{1,0,2:T(8,128)(2,1)} %bitcast.29, f32[2,512]{1,0:T(2,128)S(1)} %multiply_exponential_fusion.1, f32[96,512]{1,0:T(8,128)S(1)} %convert_element_type.24), kind=kOutput, calls=%fused_computation.14 | convolution fusion | flops 151191552 | bytes 1576960 | tf_op jit(solution)/shard_map/tro,co->trc/dot_general | solution.py:143
  27.2 0.0 reduce-scatter.3.cloned.1.call-update
  27.2 0.0 reduce-scatter.5.cloned.1.call-start
  27.2 0.0 copy-done.3
  27.3 0.0 copy-done.2
  27.3 0.1 multiply_exponential_fusion
  27.4 0.0 copy-done.1
  27.4 0.2 convert_element_type.22
  27.6 69.0 %shard_map.83 = bf16[8,96,5120]{2,1,0:T(8,128)(2,1)} custom-call(bf16[96,5120]{1,0:T(8,128)(2,1)} %panel.2), custom_call_target="tpu_custom_call" | custom-call | tf_op jit(solution)/shard_map/pallas_call | solution.py:94
  96.6 0.0 copy-start.5
  96.6 0.0 copy-start.4
  96.6 6.8 %fusion = f32[2,96,768]{2,1,0:T(8,128)} fusion(bf16[768,5120,1]{1,0,2:T(8,128)(2,1)} %bitcast.27, f32[2,5120]{1,0:T(2,128)S(1)} %multiply_exponential_fusion, f32[96,5120]{1,0:T(8,128)S(1)} %convert_element_type.22), kind=kOutput, calls=%fused_computation.1 | convolution fusion | flops 1511915520 | bytes 10461184 | tf_op jit(solution)/shard_map/tra,ca->trc/dot_general | solution.py:147
  103.5 0.0 reduce-scatter.5.cloned.1.call-update
  103.5 0.0 copy-done.5
  103.5 0.0 copy-done.4
  103.6 0.1 select_reduce_fusion
  103.7 0.1 broadcast_in_dim.35
  103.7 0.1 mul.90
  103.8 18.1 %shard_map.84 = bf16[8,96,1024]{2,1,0:T(8,128)(2,1)} custom-call(bf16[96,1024]{1,0:T(8,128)(2,1)} %panel.3), custom_call_target="tpu_custom_call" | custom-call | tf_op jit(solution)/shard_map/pallas_call | solution.py:94
  122.0 0.0 copy-start
  122.0 1.3 constant_dynamic-slice_fusion
  123.3 0.0 reduce-scatter.3.cloned.1.call-done
  123.3 4.9 %reduce-scatter.5.cloned.1.call-done = f32[2,24,768]{2,1,0:T(8,128)} async-done(((f32[2,96,768]{2,1,0:T(8,128)}), f32[2,24,768]{2,1,0:T(8,128)}) %reduce-scatter.5.cloned.1.call-update) | async-done | bytes 147472 | tf_op jit(solution)/shard_map/reduce_scatter | solution.py:149
  128.2 1.0 multiply_convert_fusion.4
  129.2 9.2 %all_gather.3 = bf16[2,96,768]{2,1,0:T(8,128)(2,1)S(1)} all-gather(bf16[2,24,768]{2,1,0:T(8,128)(2,1)S(1)} %multiply_convert_fusion.4), channel_id=1, replica_groups=mesh['pts'=8,'orb'=4] {'orb'}, dimensions={1}, use_global_device_ids=true | all-gather | bytes 368640 | tf_op jit(solution)/shard_map/all_gather | solution.py:153
  138.4 3.4 %collective-permute-start.2 = (bf16[768,512]{1,0:T(8,128)(2,1)S(1)}, bf16[768,512]{1,0:T(8,128)(2,1)S(1)}, u32[]{:S(2)}, u32[]{:S(2)}) collective-permute-start(bf16[768,512]{1,0:T(8,128)(2,1)S(1)} %bitcast.31), channel_id=1, source_target_pairs={{0,3},{4,7},{9,8},{13,12},{18,17},{22,21},{27,26},{31,30}} | collective-permute-start | bytes 2359304 | tf_op jit(solution)/shard_map/ppermute | solution.py:169
  141.8 2.2 %collective-permute-start.1 = (bf16[768,512]{1,0:T(8,128)(2,1)S(1)}, bf16[768,512]{1,0:T(8,128)(2,1)}, u32[]{:S(2)}, u32[]{:S(2)}) collective-permute-start(bf16[768,512]{1,0:T(8,128)(2,1)S(1)} %bitcast.32), channel_id=1, source_target_pairs={{0,2},{4,6},{9,11},{13,15},{18,16},{22,20},{27,25},{31,29}} | collective-permute-start | bytes 2359304 | tf_op jit(solution)/shard_map/ppermute | solution.py:169
  144.0 2.2 %collective-permute-start = (bf16[768,512]{1,0:T(8,128)(2,1)S(1)}, bf16[768,512]{1,0:T(8,128)(2,1)}, u32[]{:S(2)}, u32[]{:S(2)}) collective-permute-start(bf16[768,512]{1,0:T(8,128)(2,1)S(1)} %bitcast.33), channel_id=1, source_target_pairs={{0,1},{4,5},{9,10},{13,14},{18,19},{22,23},{27,24},{31,28}} | collective-permute-start | bytes 2359304 | tf_op jit(solution)/shard_map/ppermute | solution.py:169
  146.2 0.0 copy-done
  146.2 1.2 convolution_convert_fusion
  147.4 27.8 %shard_map.85 = bf16[8,192,1024]{2,1,0:T(8,128)(2,1)} custom-call(bf16[192,1024]{1,0:T(8,128)(2,1)} %bitcast.30), custom_call_target="tpu_custom_call" | custom-call | tf_op jit(solution)/shard_map/pallas_call | solution.py:94
  175.3 2.3 %copy.14 = bf16[2,8,96,1024]{3,2,1,0:T(8,128)(2,1)S(1)} copy(bf16[2,8,96,1024]{3,2,0,1:T(8,128)(2,1)} %bitcast.25) | data formatting | bytes 6291456 | tf_op jit(solution)/shard_map/transpose | solution.py:180
  177.6 0.0 collective-permute-done.2
  177.6 0.0 collective-permute-done.1
  177.6 0.0 collective-permute-done
  177.6 3.3 %fusion.3 = f32[512,2,1024]{2,0,1:T(8,128)S(1)} fusion(bf16[2,768,1024]{2,1,0:T(8,128)(2,1)S(1)} %bitcast.28, bf16[768,512]{1,0:T(8,128)(2,1)S(1)} %collective-permute-done.2, bf16[768,512]{1,0:T(8,128)(2,1)} %collective-permute-done.1, bf16[768,512]{1,0:T(8,128)(2,1)} %collective-permute-done, bf16[768,512]{1,0:T(8,128)(2,1)S(1)} %bitcast.34, pred[]{:T(512)S(6)} %eq.20), kind=kOutput, calls=%fused_computation.5 | convolution fusion | flops 1614151680 | bytes 10485761 | tf_op jit(solution)/shard_map/rp,trq->ptq/dot_general | solution.py:184
  180.9 5.2 %copy.16 = f32[512,2,1024]{2,1,0:T(2,128)} copy(f32[512,2,1024]{2,0,1:T(8,128)S(1)} %fusion.3) | data formatting | bytes 8388608 | tf_op jit(solution)/shard_map/rp,trq->ptq/dot_general | solution.py:184
  (3 shorter events, 0.0 us)
Async XLA Ops:
  6.5 20.7 %copy-start.3 = (f32[2]{0:T(128)S(1)}, f32[2]{0:T(128)}, u32[]{:S(2)}) copy-start(f32[2]{0:T(128)} %param.12) | copy-start | bytes 28
  6.5 20.8 %copy-start.1 = (bf16[96,5120]{1,0:T(8,128)(2,1)S(1)}, bf16[96,5120]{1,0:T(8,128)(2,1)}, u32[]{:S(2)}) copy-start(bf16[96,5120]{1,0:T(8,128)(2,1)} %panel.2) | copy-start | bytes 2949124
  6.5 20.7 %copy-start.2 = (f32[5120]{0:T(1024)S(1)}, f32[5120]{0:T(1024)}, u32[]{:S(2)}) copy-start(f32[5120]{0:T(1024)} %param.11) | copy-start | bytes 61444
  6.5 116.8 %reduce-scatter.3.cloned.1.call-start = ((), (), s32[]{:S(2)}) async-start(), calls=%async_computation.2 | async-start | bytes 737280 | tf_op jit(solution)/shard_map/reduce_scatter | solution.py:145
  27.2 101.0 %reduce-scatter.5.cloned.1.call-start = ((), (), s32[]{:S(2)}) async-start(), calls=%async_computation.3 | async-start | bytes 737280 | tf_op jit(solution)/shard_map/reduce_scatter | solution.py:149
  96.6 6.9 %copy-start.5 = (s32[8]{0:T(128)S(1)}, s32[8]{0:T(128)}, u32[]{:S(2)}) copy-start(s32[8]{0:T(128)} %constant.58.clone) | copy-start | bytes 100
  96.6 6.9 %copy-start.4 = (s32[1,8]{1,0:T(1,128)S(1)}, s32[1,8]{1,0:T(1,128)}, u32[]{:S(2)}) copy-start(s32[1,8]{1,0:T(1,128)} %param.13) | copy-start | bytes 100
  122.0 24.2 %copy-start = (bf16[8,96,1024]{2,1,0:T(8,128)(2,1)S(1)}, bf16[8,96,1024]{2,1,0:T(8,128)(2,1)}, u32[]{:S(2)}) copy-start(bf16[8,96,1024]{2,1,0:T(8,128)(2,1)} %shard_map.84) | copy-start | bytes 4718596
  138.4 39.2 %collective-permute-start.2 = (bf16[768,512]{1,0:T(8,128)(2,1)S(1)}, bf16[768,512]{1,0:T(8,128)(2,1)S(1)}, u32[]{:S(2)}, u32[]{:S(2)}) collective-permute-start(bf16[768,512]{1,0:T(8,128)(2,1)S(1)} %bitcast.31), channel_id=1, source_target_pairs={{0,3},{4,7},{9,8},{13,12},{18,17},{22,21},{27,26},{31,30}} | collective-permute-start | bytes 2359304 | tf_op jit(solution)/shard_map/ppermute | solution.py:169
  141.8 35.8 %collective-permute-start.1 = (bf16[768,512]{1,0:T(8,128)(2,1)S(1)}, bf16[768,512]{1,0:T(8,128)(2,1)}, u32[]{:S(2)}, u32[]{:S(2)}) collective-permute-start(bf16[768,512]{1,0:T(8,128)(2,1)S(1)} %bitcast.32), channel_id=1, source_target_pairs={{0,2},{4,6},{9,11},{13,15},{18,16},{22,20},{27,25},{31,29}} | collective-permute-start | bytes 2359304 | tf_op jit(solution)/shard_map/ppermute | solution.py:169
  144.0 33.6 %collective-permute-start = (bf16[768,512]{1,0:T(8,128)(2,1)S(1)}, bf16[768,512]{1,0:T(8,128)(2,1)}, u32[]{:S(2)}, u32[]{:S(2)}) collective-permute-start(bf16[768,512]{1,0:T(8,128)(2,1)S(1)} %bitcast.33), channel_id=1, source_target_pairs={{0,1},{4,5},{9,10},{13,14},{18,19},{22,23},{27,24},{31,28}} | collective-permute-start | bytes 2359304 | tf_op jit(solution)/shard_map/ppermute | solution.py:169
Sparse Core Ops, SparseCore 0:
  27.3 24.5 reduce-scatter.2
  103.6 24.5 reduce-scatter.4
